TPU v7x, 32 devices: a whole 2x2x4 slice. The times are simulated.
32 devices in a mesh: vin: 8 (over z, core), vout: 2 (over x), cell: 2 (over y).
Axes of the slice: x: 2, y: 2, z: 4, core: 2. Of those that a mesh axis runs over, the one named last changes fastest.
Arguments:
- distribution: bfloat16 [8, 13824, 4, 128], P('vout', 'vin', 'cell'), may hold values from -6 to 6
- collision: bfloat16 [13824, 13824], P('vout', 'vin'), may hold values from -1 to 3
- speeds: float32 [3, 13824], P(None, 'vout'), may hold values from 0.05 to 0.3
- directions: int32 [3, 13824], P(None, 'vout'), may hold values from 0 to 1
- cell_flags: int32 [8, 4, 128], P('vin', 'cell'), may hold values 0 or 1
Outputs:
- updated: bfloat16 [8, 13824, 4, 128], P('vin', 'vout', 'cell')
Inputs may be any that keep to these rules, and one draw needn't show every extreme that they name: `directions`: 1 means the component is positive, 0 negative. `cell_flags`: 1 marks a solid cell, where nothing is transported.
All inputs are finite; a program needn't handle non-finite values. No bound on the sum of `cell_flags` on one device may be relied on, other than what follows from the above.
Results may differ from a plain program's by a relative error of at most 0.023.
Values may be sent and summed in bfloat16 or wider, within the bound.
A program may use at most 128 MiB of HBM per device.

v0:
```python
import jax
import jax.numpy as jnp
from jax import lax
from jax.sharding import PartitionSpec as P


def with_halo(cells, sides, width):
    for axis, dim in sides:
        count = lax.axis_size(axis)
        ends = count - 1
        head = lax.slice_in_dim(cells, 0, width, axis=dim)
        tail = lax.slice_in_dim(cells, cells.shape[dim] - width, cells.shape[dim], axis=dim)
        cells = jnp.concatenate(
            [
                lax.ppermute(tail, axis, [(i, (i + 1) % count) for i in range(ends)]),
                cells,
                lax.ppermute(head, axis, [((i + 1) % count, i) for i in range(ends)]),
            ],
            axis=dim,
        )
    return cells


def transport(padded, speeds, directions, cell_flags):
    field_pad = padded.astype(jnp.float32)
    extended = jnp.pad(field_pad, ((0, 0), (0, 0), (0, 0), (1, 1)))
    center = extended[1:-1, :, 1:-1, 1:-1]
    neighbours = (
        (extended[1:-1, :, 1:-1, :-2], extended[1:-1, :, 1:-1, 2:]),
        (extended[1:-1, :, :-2, 1:-1], extended[1:-1, :, 2:, 1:-1]),
        (extended[:-2, :, 1:-1, 1:-1], extended[2:, :, 1:-1, 1:-1]),
    )
    flux_sum = jnp.zeros_like(center)
    for component in range(3):
        low_side, high_side = neighbours[component]
        positive = (directions[component] == 1)[None, :, None, None]
        upstream = jnp.where(positive, low_side, high_side)
        flux_sum = flux_sum + speeds[component][None, :, None, None] * (center - upstream)
    fluid_mask = (1 - cell_flags).astype(jnp.float32)[:, None, :, :]
    return (center - fluid_mask * flux_sum).astype(jnp.bfloat16)


def on_device(distribution, collision, speeds, directions, cell_flags):
    planes = lax.all_gather(distribution, "vout", axis=0, tiled=True)
    summed = lax.psum_scatter(
        jnp.einsum("vu,zuyx->zvyx", collision, planes, preferred_element_type=jnp.float32).astype(
            jnp.bfloat16
        ),
        "vin",
        scatter_dimension=0,
        tiled=True,
    )
    padded = with_halo(summed, (("vin", 0), ("cell", 2)), 1)
    return transport(padded, speeds, directions, cell_flags)


def solution(mesh):
    return jax.shard_map(
        on_device,
        mesh=mesh,
        in_specs=(
            P("vout", "vin", "cell", None),
            P("vout", "vin"),
            P(None, "vout"),
            P(None, "vout"),
            P("vin", "cell", None),
        ),
        out_specs=P("vin", "vout", "cell", None),
        check_vma=False,
    )
```

profile of v0, /device:TPU:8, one launch (start us, length us, event | category | flops | bytes accessed | tf_op | source)
XLA Modules:
  0.0 663.2 jit_solution(15532418143179087051)
XLA Ops:
  6.5 4.2 copy.8
  10.8 0.0 all-gather.2.cloned.1.call-update
  10.8 0.0 reduce-scatter.2.cloned.1.call-start
  10.9 90.5 %all-gather.2.cloned.1.call-done = bf16[8,1728,2,128]{3,1,2,0:T(8,128)(2,1)} async-done(((bf16[4,1728,2,128]{3,1,2,0:T(8,128)(2,1)}), bf16[8,1728,2,128]{3,1,2,0:T(8,128)(2,1)}) %all-gather.2.cloned.1.call-update) | async-done | bytes 7077904 | tf_op jit(solution)/shard_map/all_gather | solution.py:44
  101.4 59.2 %convert_bitcast_fusion = bf16[8,6912,2,128]{1,3,2,0:T(8,128)(2,1)} fusion(bf16[8,1728,2,128]{3,1,2,0:T(8,128)(2,1)} %all-gather.2.cloned.1.call-done, bf16[6912,1728]{0,1:T(8,128)(2,1)} %param.6), kind=kOutput, calls=%fused_computation.2 | convolution fusion | flops 48936517632 | bytes 59277312 | tf_op jit(solution)/shard_map/vu,zuyx->zvyx/dot_general | solution.py:46
  160.6 0.0 reduce-scatter.2.cloned.1.call-update
  160.6 274.1 %reduce-scatter.2.cloned.1.call-done = bf16[1,6912,2,128]{1,3,2,0:T(8,128)(2,1)} async-done(((bf16[8,6912,2,128]{1,3,2,0:T(8,128)(2,1)}), bf16[1,6912,2,128]{1,3,2,0:T(8,128)(2,1)}) %reduce-scatter.2.cloned.1.call-update) | async-done | bytes 3538960 | tf_op jit(solution)/shard_map/reduce_scatter | solution.py:45
  434.7 3.4 collective-permute-start
  438.1 2.4 collective-permute-start.1
  440.5 37.4 %collective-permute-done = bf16[1,6912,2,128]{1,3,2,0:T(8,128)(2,1)S(1)} collective-permute-done((bf16[1,6912,2,128]{1,3,2,0:T(8,128)(2,1)}, bf16[1,6912,2,128]{1,3,2,0:T(8,128)(2,1)S(1)}, u32[]{:S(2)}, u32[]{:S(2)}) %collective-permute-start) | collective-permute-done | bytes 3538976 | tf_op jit(solution)/shard_map/ppermute | solution.py:15
  478.0 2.0 constant_dynamic-update-slice_fusion.2
  479.9 2.0 constant_dynamic-update-slice_fusion.1
  481.9 0.0 collective-permute-done.1
  481.9 2.0 constant_dynamic-update-slice_fusion
  483.9 8.8 %fusion.16 = (bf16[3,6912,1,128]{1,3,2,0:T(8,128)(2,1)}, bf16[3,6912,1,128]{1,3,2,0:T(8,128)(2,1)}) fusion(bf16[3,6912,2,128]{1,3,2,0:T(8,128)(2,1)} %constant_dynamic-update-slice_fusion), kind=kLoop, calls=%fused_computation.30 | loop fusion | bytes 21233664 | tf_op jit(solution)/shard_map/slice | solution.py:12
  492.7 3.8 collective-permute-start.2
  496.5 1.5 collective-permute-start.3
  498.0 0.2 slice_reduce_fusion.2
  498.2 0.3 compare_reduce_fusion.2
  498.5 111.5 %collective-permute-done.2 = bf16[3,6912,1,128]{1,3,2,0:T(8,128)(2,1)S(1)} collective-permute-done((bf16[3,6912,1,128]{1,3,2,0:T(8,128)(2,1)}, bf16[3,6912,1,128]{1,3,2,0:T(8,128)(2,1)S(1)}, u32[]{:S(2)}, u32[]{:S(2)}) %collective-permute-start.2) | collective-permute-done | bytes 5308448 | tf_op jit(solution)/shard_map/ppermute | solution.py:15
  610.1 4.3 collective-permute-done.3
  614.4 17.8 %maximum_convert_fusion = f32[3,6912,4,128]{1,3,2,0:T(8,128)} fusion(bf16[3,6912,1,128]{1,3,2,0:T(8,128)(2,1)S(1)} %collective-permute-done.3, bf16[3,6912,2,128]{1,3,2,0:T(8,128)(2,1)} %constant_dynamic-update-slice_fusion, bf16[3,6912,1,128]{1,3,2,0:T(8,128)(2,1)S(1)} %collective-permute-done.2), kind=kLoop, calls=%fused_computation.5 | loop fusion | flops 31850496 | bytes 63700992 | tf_op jit(solution)/shard_map/convert_element_type | solution.py:25
  632.3 17.6 %fusion.15 = bf16[1,6912,2,128]{1,3,2,0:T(8,128)(2,1)S(1)} fusion(f32[3,6912,4,128]{1,3,2,0:T(8,128)} %maximum_convert_fusion, f32[6912]{0:T(1024)S(1)} %get-tuple-element.9, f32[6912]{0:T(1024)S(1)} %get-tuple-element.10, f32[6912]{0:T(1024)S(1)} %get-tuple-element.8, f32[2,128]{1,0:T(2,128)S(1)} %convert_bitcast_fusion.1, ...), kind=kLoop, calls=%fused_computation.19 | loop fusion | flops 24772608 | bytes 81500416 | tf_op jit(solution)/shard_map/convert_element_type | solution.py:40
  649.9 6.5 copy.9
  (10 shorter events, 0.0 us)
Async XLA Ops:
  6.5 94.8 %all-gather.2.cloned.1.call-start = ((), (), s32[]{:S(2)}) async-start(), calls=%async_computation.1 | async-start | bytes 10616832 | tf_op jit(solution)/shard_map/all_gather | solution.py:44
  10.8 423.9 %reduce-scatter.2.cloned.1.call-start = ((), (), s32[]{:S(2)}) async-start(), calls=%async_computation.2 | async-start | bytes 31850496 | tf_op jit(solution)/shard_map/reduce_scatter | solution.py:45
  434.7 45.2 %copy-start = (bf16[1,6912,2,128]{1,3,2,0:T(8,128)(2,1)S(1)}, bf16[1,6912,2,128]{1,3,2,0:T(8,128)(2,1)}, u32[]{:S(2)}) copy-start(bf16[1,6912,2,128]{1,3,2,0:T(8,128)(2,1)} %reduce-scatter.2.cloned.1.call-done) | copy-start | bytes 10616836
  434.7 43.3 %collective-permute-start = (bf16[1,6912,2,128]{1,3,2,0:T(8,128)(2,1)}, bf16[1,6912,2,128]{1,3,2,0:T(8,128)(2,1)S(1)}, u32[]{:S(2)}, u32[]{:S(2)}) collective-permute-start(bf16[1,6912,2,128]{1,3,2,0:T(8,128)(2,1)} %reduce-scatter.2.cloned.1.call-done), channel_id=1, source_target_pairs={{0,4},{4,8},{8,12},{12,16},{16,20},{20,24},{24,28},{1,5},{5,9},{9,... | collective-permute-start | bytes 10616840 | tf_op jit(solution)/shard_map/ppermute | solution.py:15
  438.1 43.9 %collective-permute-start.1 = (bf16[1,6912,2,128]{1,3,2,0:T(8,128)(2,1)}, bf16[1,6912,2,128]{1,3,2,0:T(8,128)(2,1)S(1)}, u32[]{:S(2)}, u32[]{:S(2)}) collective-permute-start(bf16[1,6912,2,128]{1,3,2,0:T(8,128)(2,1)} %reduce-scatter.2.cloned.1.call-done), channel_id=1, source_target_pairs={{4,0},{8,4},{12,8},{16,12},{20,16},{24,20},{28,24},{5,1},{9,5},{13... | collective-permute-start | bytes 10616840 | tf_op jit(solution)/shard_map/ppermute | solution.py:17
  483.9 14.1 %copy-start.2 = (f32[3,6912]{1,0:T(4,128)S(1)}, f32[3,6912]{1,0:T(4,128)}, u32[]{:S(2)}) copy-start(f32[3,6912]{1,0:T(4,128)} %param.7) | copy-start | bytes 248836
  483.9 14.3 %copy-start.1 = (s32[3,6912]{1,0:T(4,128)S(1)}, s32[3,6912]{1,0:T(4,128)}, u32[]{:S(2)}) copy-start(s32[3,6912]{1,0:T(4,128)} %param.8) | copy-start | bytes 248836
  483.9 14.6 %copy-start.3 = (s32[1,2,128]{2,1,0:T(2,128)S(1)}, s32[1,2,128]{2,1,0:T(2,128)}, u32[]{:S(2)}) copy-start(s32[1,2,128]{2,1,0:T(2,128)} %param.9) | copy-start | bytes 3076
  492.7 117.4 %collective-permute-start.2 = (bf16[3,6912,1,128]{1,3,2,0:T(8,128)(2,1)}, bf16[3,6912,1,128]{1,3,2,0:T(8,128)(2,1)S(1)}, u32[]{:S(2)}, u32[]{:S(2)}) collective-permute-start(bf16[3,6912,1,128]{1,3,2,0:T(8,128)(2,1)} %get-tuple-element.11), channel_id=1, source_target_pairs={{0,1},{2,3},{4,5},{6,7},{8,9},{10,11},{12,13},{14,15},{16,17},{18,... | collective-permute-start | bytes 15925256 | tf_op jit(solution)/shard_map/ppermute | solution.py:15
  496.5 117.9 %collective-permute-start.3 = (bf16[3,6912,1,128]{1,3,2,0:T(8,128)(2,1)}, bf16[3,6912,1,128]{1,3,2,0:T(8,128)(2,1)S(1)}, u32[]{:S(2)}, u32[]{:S(2)}) collective-permute-start(bf16[3,6912,1,128]{1,3,2,0:T(8,128)(2,1)} %get-tuple-element.12), channel_id=1, source_target_pairs={{1,0},{3,2},{5,4},{7,6},{9,8},{11,10},{13,12},{15,14},{17,16},{19,... | collective-permute-start | bytes 15925256 | tf_op jit(solution)/shard_map/ppermute | solution.py:17
Sparse Core Ops, SparseCore 0:
  10.9 90.3 all-gather.1
  160.8 273.8 reduce-scatter.1
where the time goes:
time: 664 us; the launch traced here: 663 us
  waiting for transfers between devices  518 us (78%)
  matrix products  59.2 us (9%)
  other arithmetic  35.7 us (5%)
  local copies, waits for them, and re-layouts  25.8 us (4%)
  between operations  13.5 us (2%)
  starting transfers between devices  11.1 us (2%)
    reduce_scatter x1, waiting for transfers between devices, on_device(): lax.psum_scatter(jnp.einsum('vu,zuyx->zvyx', collision, planes, preferred...  274 us
    ppermute x2, waiting for transfers between devices, with_halo(): lax.ppermute(tail, axis, [(i, (i + 1) % count) for i in range(ends)])  149 us
    all_gather x1, waiting for transfers between devices, on_device(): planes = lax.all_gather(distribution, 'vout', axis=0, tiled=True)  90.5 us
    dot_general x1, matrix products, on_device(): jnp.einsum('vu,zuyx->zvyx', collision, planes, preferred_element_type=jnp...  59.2 us
    convert_element_type x1, other arithmetic, transport(): field_pad = padded.astype(jnp.float32)  17.8 us
    convert_element_type x1, other arithmetic, transport(): return (center - fluid_mask * flux_sum).astype(jnp.bfloat16)  17.6 us
  transfers between devices with their start and end apart: 6, of which 5 were waited for; matrix products, arithmetic and copies ran while one was open for 1% of the time, Pallas kernels for 0%

commit v1 on v0

v1 whole, which is shorter than its diff:
```python
import jax
import jax.numpy as jnp
from jax import lax
from jax.sharding import PartitionSpec as P

CHUNKS = 4


def from_lower(values, axis):
    ends = lax.axis_size(axis) - 1
    return lax.ppermute(values, axis, [(i, i + 1) for i in range(ends)])


def from_higher(values, axis):
    ends = lax.axis_size(axis) - 1
    return lax.ppermute(values, axis, [(i + 1, i) for i in range(ends)])


def shifted(values, step):
    edge = jnp.zeros_like(values[:, :1])
    if step > 0:
        return jnp.concatenate([edge, values[:, :-1]], axis=1)
    return jnp.concatenate([values[:, 1:], edge], axis=1)


def transport(center, neighbours, speeds, positive, fluid):
    middle = center.astype(jnp.float32)
    flux = jnp.zeros_like(middle)
    for component, (low, high) in enumerate(neighbours):
        upstream = jnp.where(positive[component][:, None], low, high).astype(jnp.float32)
        flux = flux + speeds[component][:, None] * (middle - upstream)
    return (middle - fluid[None, :] * flux).astype(jnp.bfloat16)


def on_device(distribution, collision, speeds, directions, cell_flags):
    rows = distribution.shape[2]
    velocities = collision.shape[0]
    chunk = velocities // CHUNKS
    planes = [
        lax.all_gather(distribution[:, :, row, :], "vout", axis=0, tiled=True)
        for row in range(rows)
    ]
    fluid = (1 - cell_flags[0]).astype(jnp.float32)
    relaxed = [[None] * rows for _ in range(CHUNKS)]
    for row in range(rows):
        for part in range(CHUNKS):
            block = lax.slice_in_dim(collision, part * chunk, (part + 1) * chunk, axis=0)
            partial = jnp.einsum(
                "vu,zux->zvx", block, planes[row], preferred_element_type=jnp.float32
            ).astype(jnp.bfloat16)
            relaxed[part][row] = lax.psum_scatter(
                partial, "vin", scatter_dimension=0, tiled=True
            )[0]
    outs = []
    for part in range(CHUNKS):
        cells = relaxed[part]
        own = slice(part * chunk, (part + 1) * chunk)
        positive = directions[:, own] == 1
        pace = speeds[:, own]
        before = from_lower(cells[-1], "cell")
        after = from_higher(cells[0], "cell")
        column = [before, *cells, after]
        done = []
        for row in range(rows):
            center = cells[row]
            neighbours = (
                (shifted(center, 1), shifted(center, -1)),
                (column[row], column[row + 2]),
                (from_lower(center, "vin"), from_higher(center, "vin")),
            )
            done.append(transport(center, neighbours, pace, positive, fluid[row]))
        outs.append(jnp.stack(done, axis=1))
    return jnp.concatenate(outs, axis=0)[None]


def solution(mesh):
    return jax.shard_map(
        on_device,
        mesh=mesh,
        in_specs=(
            P("vout", "vin", "cell", None),
            P("vout", "vin"),
            P(None, "vout"),
            P(None, "vout"),
            P("vin", "cell", None),
        ),
        out_specs=P("vin", "vout", "cell", None),
        check_vma=False,
    )
```

time: 664 us -> 629 us (0.947); the launches traced: 663 us -> 619 us
  waiting for transfers between devices: 518 us -> 333 us
  starting transfers between devices: 11.1 us -> 69 us
  matrix products: 59.2 us -> 102 us
  local copies, waits for them, and re-layouts: 25.8 us -> 64.7 us
    ppermute x4 -> x24, waiting for transfers between devices: 153 us -> 7.82 us  [the longest x12 7.08 us: from_lower(): return lax.ppermute(values, axis, [(i, i + 1) for i in range(ends)])]
    ppermute x4 -> x24, starting transfers between devices: 11.1 us -> 67.9 us  [the longest x12 37.9 us: from_lower(): return lax.ppermute(values, axis, [(i, i + 1) for i in range(ends)])]
    dot_general x1 -> x8, matrix products: 59.2 us -> 102 us  [on_device(): jnp.einsum('vu,zux->zvx', block, planes[row], preferred_element_type=jnp....]
    convert_element_type x2 -> x1, other arithmetic: 35.4 us -> 0.01 us  [on_device(): fluid = (1 - cell_flags[0]).astype(jnp.float32)]
    reduce_scatter x1 -> x8, waiting for transfers between devices: 274 us -> 240 us  [on_device(): lax.psum_scatter(partial, 'vin', scatter_dimension=0, tiled=True)[0]]
    broadcast_in_dim x0 -> x1, local copies, waits for them, and re-layouts: none -> 30 us  [on_device(): return jnp.concatenate(outs, axis=0)[None]]
    another operation x0 -> x8, other arithmetic: none -> 22.3 us  [on_device(): outs.append(jnp.stack(done, axis=1))]
    slice x2 -> x14, local copies, waits for them, and re-layouts: 9.03 us -> 26.6 us  [the longest x8 15.4 us: shifted(): return jnp.concatenate([edge, values[:, :-1]], axis=1)]
  transfers between devices with their start and end apart: 6 -> 34, of which waited for: 5 -> 10; matrix products, arithmetic and copies ran while one was open for 1% -> 23% of each run, Pallas kernels for 0% -> 0%
where the time goes in v1:
time: 629 us; the launch traced here: 619 us
  waiting for transfers between devices  333 us (53%)
  matrix products  102 us (16%)
  starting transfers between devices  69 us (11%)
  local copies, waits for them, and re-layouts  64.7 us (10%)
  other arithmetic  34.9 us (6%)
  between operations  15 us (2%)
    reduce_scatter x8, waiting for transfers between devices, on_device(): lax.psum_scatter(partial, 'vin', scatter_dimension=0, tiled=True)[0]  240 us
    dot_general x8, matrix products, on_device(): jnp.einsum('vu,zux->zvx', block, planes[row], preferred_element_type=jnp....  102 us
    all_gather x2, waiting for transfers between devices, on_device(): lax.all_gather(distribution[:, :, row, :], 'vout', axis=0, tiled=True)  85.4 us
    ppermute x12, starting transfers between devices, from_lower(): return lax.ppermute(values, axis, [(i, i + 1) for i in range(ends)])  37.9 us
    broadcast_in_dim x1, local copies, waits for them, and re-layouts, on_device(): return jnp.concatenate(outs, axis=0)[None]  30 us
    ppermute x12, starting transfers between devices, from_higher(): return lax.ppermute(values, axis, [(i + 1, i) for i in range(ends)])  30 us
    another operation x8, other arithmetic, on_device(): outs.append(jnp.stack(done, axis=1))  22.3 us
    slice x8, local copies, waits for them, and re-layouts, shifted(): return jnp.concatenate([edge, values[:, :-1]], axis=1)  15.4 us
  transfers between devices with their start and end apart: 34, of which 10 were waited for; matrix products, arithmetic and copies ran while one was open for 23% of the time, Pallas kernels for 0%

profile of v1, /device:TPU:8, one launch (start us, length us, event | category | flops | bytes accessed | tf_op | source)
XLA Modules:
  0.0 619.0 jit_solution(6708715030905493566)
XLA Ops:
  6.5 7.7 %fusion.160 = (bf16[4,1728,1,128]{3,2,1,0:T(2,128)(2,1)S(1)}, bf16[4,1728,1,128]{3,2,1,0:T(2,128)(2,1)S(1)}) fusion(bf16[4,1728,2,128]{3,2,1,0:T(2,128)(2,1)} %param.5), kind=kLoop, calls=%fused_computation.176 | loop fusion | bytes 7077888 | tf_op jit(solution)/shard_map/slice | solution.py:40
  17.3 49.1 %all-gather.7.cloned.1.call-done = bf16[8,1728,1,128]{3,1,2,0:T(8,128)(2,1)} async-done(((bf16[4,1728,1,128]{3,1,2,0:T(8,128)(2,1)}), bf16[8,1728,1,128]{3,1,2,0:T(8,128)(2,1)}) %all-gather.7.cloned.1.call-update) | async-done | bytes 3538960 | tf_op jit(solution)/shard_map/all_gather | solution.py:40
  66.4 14.6 %fusion.56 = bf16[8,1728,128]{2,1,0:T(8,128)(2,1)} fusion(bf16[8,1728,1,128]{3,1,2,0:T(8,128)(2,1)} %all-gather.7.cloned.1.call-done, bf16[6912,1728]{0,1:T(8,128)(2,1)} %param.6), kind=kOutput, calls=%fused_computation.41 | convolution fusion | flops 6117064704 | bytes 13271040 | tf_op jit(solution)/shard_map/vu,zux->zvx/dot_general | solution.py:48
  81.0 36.3 %all-gather.5.cloned.1.call-done = bf16[8,1728,1,128]{3,1,2,0:T(8,128)(2,1)} async-done(((bf16[4,1728,1,128]{3,1,2,0:T(8,128)(2,1)}), bf16[8,1728,1,128]{3,1,2,0:T(8,128)(2,1)}) %all-gather.5.cloned.1.call-update) | async-done | bytes 3538960 | tf_op jit(solution)/shard_map/all_gather | solution.py:40
  117.3 14.6 %fusion.61 = bf16[8,1728,128]{2,1,0:T(8,128)(2,1)} fusion(bf16[8,1728,1,128]{3,1,2,0:T(8,128)(2,1)} %all-gather.5.cloned.1.call-done, bf16[6912,1728]{0,1:T(8,128)(2,1)} %param.6), kind=kOutput, calls=%fused_computation.42 | convolution fusion | flops 6117064704 | bytes 13271040 | tf_op jit(solution)/shard_map/vu,zux->zvx/dot_general | solution.py:48
  134.0 10.9 %fusion.66 = bf16[8,1728,128]{2,1,0:T(8,128)(2,1)} fusion(bf16[8,1728,1,128]{3,1,2,0:T(8,128)(2,1)S(1)} %copy-done.43, bf16[6912,1728]{0,1:T(8,128)(2,1)} %param.6), kind=kOutput, calls=%fused_computation.43 | convolution fusion | flops 6117064704 | bytes 13271040 | tf_op jit(solution)/shard_map/vu,zux->zvx/dot_general | solution.py:48
  144.9 11.5 %fusion.71 = bf16[8,1728,128]{2,1,0:T(8,128)(2,1)} fusion(bf16[8,1728,1,128]{3,1,2,0:T(8,128)(2,1)} %all-gather.5.cloned.1.call-done, bf16[6912,1728]{0,1:T(8,128)(2,1)} %param.6), kind=kOutput, calls=%fused_computation.44 | convolution fusion | flops 6117064704 | bytes 13271040 | tf_op jit(solution)/shard_map/vu,zux->zvx/dot_general | solution.py:48
  156.5 14.2 %fusion.76 = bf16[8,1728,128]{2,1,0:T(8,128)(2,1)} fusion(bf16[8,1728,1,128]{3,1,2,0:T(8,128)(2,1)S(1)} %copy-done.43, bf16[6912,1728]{0,1:T(8,128)(2,1)} %param.6), kind=kOutput, calls=%fused_computation.45 | convolution fusion | flops 6117064704 | bytes 13271040 | tf_op jit(solution)/shard_map/vu,zux->zvx/dot_general | solution.py:48
  170.9 14.7 %fusion.81 = bf16[8,1728,128]{2,1,0:T(8,128)(2,1)} fusion(bf16[8,1728,1,128]{3,1,2,0:T(8,128)(2,1)} %all-gather.5.cloned.1.call-done, bf16[6912,1728]{0,1:T(8,128)(2,1)} %param.6), kind=kOutput, calls=%fused_computation.46 | convolution fusion | flops 6117064704 | bytes 13271040 | tf_op jit(solution)/shard_map/vu,zux->zvx/dot_general | solution.py:48
  185.7 10.9 %fusion.86 = bf16[8,1728,128]{2,1,0:T(8,128)(2,1)} fusion(bf16[8,1728,1,128]{3,1,2,0:T(8,128)(2,1)S(1)} %copy-done.43, bf16[6912,1728]{0,1:T(8,128)(2,1)} %param.6), kind=kOutput, calls=%fused_computation.47 | convolution fusion | flops 6117064704 | bytes 13271040 | tf_op jit(solution)/shard_map/vu,zux->zvx/dot_general | solution.py:48
  198.7 10.9 %fusion.91 = bf16[8,1728,128]{2,1,0:T(8,128)(2,1)} fusion(bf16[8,1728,1,128]{3,1,2,0:T(8,128)(2,1)S(1)} %copy-done.44, bf16[6912,1728]{0,1:T(8,128)(2,1)} %param.6), kind=kOutput, calls=%fused_computation.48 | convolution fusion | flops 6117064704 | bytes 13271040 | tf_op jit(solution)/shard_map/vu,zux->zvx/dot_general | solution.py:48
  231.9 25.8 %reduce-scatter.19.cloned.1.call-done = bf16[1,1728,128]{2,1,0:T(8,128)(2,1)} async-done(((bf16[8,1728,128]{2,1,0:T(8,128)(2,1)}), bf16[1,1728,128]{2,1,0:T(8,128)(2,1)}) %reduce-scatter.19.cloned.1.call-update) | async-done | bytes 442384 | tf_op jit(solution)/shard_map/reduce_scatter | solution.py:51
  259.9 42.6 %reduce-scatter.17.cloned.1.call-done = bf16[1,1728,128]{2,1,0:T(8,128)(2,1)} async-done(((bf16[8,1728,128]{2,1,0:T(8,128)(2,1)}), bf16[1,1728,128]{2,1,0:T(8,128)(2,1)}) %reduce-scatter.17.cloned.1.call-update) | async-done | bytes 442384 | tf_op jit(solution)/shard_map/reduce_scatter | solution.py:51
  304.7 42.4 %reduce-scatter.15.cloned.1.call-done = bf16[1,1728,128]{2,1,0:T(8,128)(2,1)} async-done(((bf16[8,1728,128]{2,1,0:T(8,128)(2,1)}), bf16[1,1728,128]{2,1,0:T(8,128)(2,1)}) %reduce-scatter.15.cloned.1.call-update) | async-done | bytes 442384 | tf_op jit(solution)/shard_map/reduce_scatter | solution.py:51
  349.4 42.5 %reduce-scatter.13.cloned.1.call-done = bf16[1,1728,128]{2,1,0:T(8,128)(2,1)} async-done(((bf16[8,1728,128]{2,1,0:T(8,128)(2,1)}), bf16[1,1728,128]{2,1,0:T(8,128)(2,1)}) %reduce-scatter.13.cloned.1.call-update) | async-done | bytes 442384 | tf_op jit(solution)/shard_map/reduce_scatter | solution.py:51
  393.3 43.3 %reduce-scatter.11.cloned.1.call-done = bf16[1,1728,128]{2,1,0:T(8,128)(2,1)} async-done(((bf16[8,1728,128]{2,1,0:T(8,128)(2,1)}), bf16[1,1728,128]{2,1,0:T(8,128)(2,1)}) %reduce-scatter.11.cloned.1.call-update) | async-done | bytes 442384 | tf_op jit(solution)/shard_map/reduce_scatter | solution.py:51
  438.0 43.2 %reduce-scatter.9.cloned.1.call-done = bf16[1,1728,128]{2,1,0:T(8,128)(2,1)} async-done(((bf16[8,1728,128]{2,1,0:T(8,128)(2,1)}), bf16[1,1728,128]{2,1,0:T(8,128)(2,1)}) %reduce-scatter.9.cloned.1.call-update) | async-done | bytes 442384 | tf_op jit(solution)/shard_map/reduce_scatter | solution.py:51
  492.4 4.7 fusion.152
  504.5 4.4 fusion.153
  530.4 4.6 collective-permute-start.6
  552.0 4.8 collective-permute-start
  559.9 7.1 %collective-permute-done = bf16[1728,128]{1,0:T(8,128)(2,1)S(1)} collective-permute-done((bf16[1728,128]{1,0:T(8,128)(2,1)S(1)}, bf16[1728,128]{1,0:T(8,128)(2,1)S(1)}, u32[]{:S(2)}, u32[]{:S(2)}) %collective-permute-start) | collective-permute-done | bytes 442400 | tf_op jit(solution)/shard_map/ppermute | solution.py:11
  569.1 12.5 %maximum_bitcast_fusion = bf16[1,6912,2,128]{3,1,2,0:T(8,128)(2,1)S(1)} fusion(bf16[1728,1,128]{2,0,1:T(8,128)(2,1)S(1)} %fusion.152, bf16[1728,1,128]{2,0,1:T(8,128)(2,1)S(1)} %fusion.153, bf16[1728,1,128]{2,0,1:T(8,128)(2,1)S(1)} %fusion.154, bf16[1728,1,128]{2,0,1:T(8,128)(2,1)S(1)} %fusion.155, bf16[1728,1,128]{2,0,1:T(8,128)(2,1)S(1)} %fusion.156, ...), kind=kLoop, calls=%fused_computation.32 | loop fusion | flops 28311552 | bytes 7077888 | tf_op jit(solution)/shard_map/broadcast_in_dim | solution.py:73
  581.7 30.0 %copy.19 = bf16[1,6912,2,128]{3,2,1,0:T(2,128)(2,1)} copy(bf16[1,6912,2,128]{3,1,2,0:T(8,128)(2,1)S(1)} %maximum_bitcast_fusion) | data formatting | bytes 7077888 | tf_op jit(solution)/shard_map/broadcast_in_dim | solution.py:73
  (181 shorter events, 100.8 us)
Async XLA Ops:
  6.5 59.8 %all-gather.7.cloned.1.call-start = ((), (), s32[]{:S(2)}) async-start(), calls=%async_computation.17 | async-start | bytes 5308416 | tf_op jit(solution)/shard_map/all_gather | solution.py:40
  15.7 101.6 %all-gather.5.cloned.1.call-start = ((), (), s32[]{:S(2)}) async-start(), calls=%async_computation.16 | async-start | bytes 5308416 | tf_op jit(solution)/shard_map/all_gather | solution.py:40
  17.2 197.5 %reduce-scatter.23.cloned.1.call-start = ((), (), s32[]{:S(2)}) async-start(), calls=%async_computation.15 | async-start | bytes 3981312 | tf_op jit(solution)/shard_map/reduce_scatter | solution.py:51
  81.0 139.3 %reduce-scatter.21.cloned.1.call-start = ((), (), s32[]{:S(2)}) async-start(), calls=%async_computation.14 | async-start | bytes 3981312 | tf_op jit(solution)/shard_map/reduce_scatter | solution.py:51
  132.0 125.7 %reduce-scatter.19.cloned.1.call-start = ((), (), s32[]{:S(2)}) async-start(), calls=%async_computation.13 | async-start | bytes 3981312 | tf_op jit(solution)/shard_map/reduce_scatter | solution.py:51
  144.9 157.6 %reduce-scatter.17.cloned.1.call-start = ((), (), s32[]{:S(2)}) async-start(), calls=%async_computation.12 | async-start | bytes 3981312 | tf_op jit(solution)/shard_map/reduce_scatter | solution.py:51
  156.4 190.7 %reduce-scatter.15.cloned.1.call-start = ((), (), s32[]{:S(2)}) async-start(), calls=%async_computation.11 | async-start | bytes 3981312 | tf_op jit(solution)/shard_map/reduce_scatter | solution.py:51
  170.7 221.2 %reduce-scatter.13.cloned.1.call-start = ((), (), s32[]{:S(2)}) async-start(), calls=%async_computation.10 | async-start | bytes 3981312 | tf_op jit(solution)/shard_map/reduce_scatter | solution.py:51
  185.7 250.9 %reduce-scatter.11.cloned.1.call-start = ((), (), s32[]{:S(2)}) async-start(), calls=%async_computation.9 | async-start | bytes 3981312 | tf_op jit(solution)/shard_map/reduce_scatter | solution.py:51
  196.7 284.6 %reduce-scatter.9.cloned.1.call-start = ((), (), s32[]{:S(2)}) async-start(), calls=%async_computation.8 | async-start | bytes 3981312 | tf_op jit(solution)/shard_map/reduce_scatter | solution.py:51
  214.7 268.0 %collective-permute-start.22 = (bf16[1728,128]{1,0:T(8,128)(2,1)}, bf16[1728,128]{1,0:T(8,128)(2,1)}, u32[]{:S(2)}, u32[]{:S(2)}) collective-permute-start(bf16[1728,128]{1,0:T(8,128)(2,1)} %bitcast.180), channel_id=1, source_target_pairs={{0,4},{4,8},{8,12},{12,16},{16,20},{20,24},{24,28},{1,5},{5,9},{9,... | collective-permute-start | bytes 1327112 | tf_op jit(solution)/shard_map/ppermute | solution.py:11
  216.6 269.9 %collective-permute-start.23 = (bf16[1728,128]{1,0:T(8,128)(2,1)}, bf16[1728,128]{1,0:T(8,128)(2,1)}, u32[]{:S(2)}, u32[]{:S(2)}) collective-permute-start(bf16[1728,128]{1,0:T(8,128)(2,1)} %bitcast.181), channel_id=1, source_target_pairs={{4,0},{8,4},{12,8},{16,12},{20,16},{24,20},{28,24},{5,1},{9,5},{13... | collective-permute-start | bytes 1327112 | tf_op jit(solution)/shard_map/ppermute | solution.py:16
  220.3 270.1 %collective-permute-start.21 = (bf16[1728,128]{1,0:T(8,128)(2,1)}, bf16[1728,128]{1,0:T(8,128)(2,1)}, u32[]{:S(2)}, u32[]{:S(2)}) collective-permute-start(bf16[1728,128]{1,0:T(8,128)(2,1)} %bitcast.184), channel_id=1, source_target_pairs={{1,0},{3,2},{5,4},{7,6},{9,8},{11,10},{13,12},{15,14},{17,16},{19,... | collective-permute-start | bytes 1327112 | tf_op jit(solution)/shard_map/ppermute | solution.py:16
  221.6 275.6 %collective-permute-start.19 = (bf16[1728,128]{1,0:T(8,128)(2,1)}, bf16[1728,128]{1,0:T(8,128)(2,1)}, u32[]{:S(2)}, u32[]{:S(2)}) collective-permute-start(bf16[1728,128]{1,0:T(8,128)(2,1)} %bitcast.185), channel_id=1, source_target_pairs={{0,4},{4,8},{8,12},{12,16},{16,20},{20,24},{24,28},{1,5},{5,9},{9,... | collective-permute-start | bytes 1327112 | tf_op jit(solution)/shard_map/ppermute | solution.py:11
  223.5 275.0 %collective-permute-start.20 = (bf16[1728,128]{1,0:T(8,128)(2,1)}, bf16[1728,128]{1,0:T(8,128)(2,1)}, u32[]{:S(2)}, u32[]{:S(2)}) collective-permute-start(bf16[1728,128]{1,0:T(8,128)(2,1)} %bitcast.186), channel_id=1, source_target_pairs={{4,0},{8,4},{12,8},{16,12},{20,16},{24,20},{28,24},{5,1},{9,5},{13... | collective-permute-start | bytes 1327112 | tf_op jit(solution)/shard_map/ppermute | solution.py:16
  482.7 18.5 %collective-permute-start.18 = (bf16[1728,128]{1,0:T(8,128)(2,1)S(1)}, bf16[1728,128]{1,0:T(8,128)(2,1)S(1)}, u32[]{:S(2)}, u32[]{:S(2)}) collective-permute-start(bf16[1728,128]{1,0:T(8,128)(2,1)S(1)} %bitcast.183), channel_id=1, source_target_pairs={{0,1},{2,3},{4,5},{6,7},{8,9},{10,11},{12,13},{14,15},{16,17},{18,... | collective-permute-start | bytes 1327112 | tf_op jit(solution)/shard_map/ppermute | solution.py:11
  486.5 22.4 %collective-permute-start.16 = (bf16[1728,128]{1,0:T(8,128)(2,1)S(1)}, bf16[1728,128]{1,0:T(8,128)(2,1)S(1)}, u32[]{:S(2)}, u32[]{:S(2)}) collective-permute-start(bf16[1728,128]{1,0:T(8,128)(2,1)S(1)} %bitcast.173), channel_id=1, source_target_pairs={{0,4},{4,8},{8,12},{12,16},{16,20},{20,24},{24,28},{1,5},{5,9},{9,... | collective-permute-start | bytes 1327112 | tf_op jit(solution)/shard_map/ppermute | solution.py:11
  490.4 22.8 %collective-permute-start.17 = (bf16[1728,128]{1,0:T(8,128)(2,1)S(1)}, bf16[1728,128]{1,0:T(8,128)(2,1)S(1)}, u32[]{:S(2)}, u32[]{:S(2)}) collective-permute-start(bf16[1728,128]{1,0:T(8,128)(2,1)S(1)} %bitcast.174), channel_id=1, source_target_pairs={{4,0},{8,4},{12,8},{16,12},{20,16},{24,20},{28,24},{5,1},{9,5},{13... | collective-permute-start | bytes 1327112 | tf_op jit(solution)/shard_map/ppermute | solution.py:16
  498.5 22.7 %collective-permute-start.13 = (bf16[1728,128]{1,0:T(8,128)(2,1)S(1)}, bf16[1728,128]{1,0:T(8,128)(2,1)S(1)}, u32[]{:S(2)}, u32[]{:S(2)}) collective-permute-start(bf16[1728,128]{1,0:T(8,128)(2,1)S(1)} %bitcast.178), channel_id=1, source_target_pairs={{0,4},{4,8},{8,12},{12,16},{16,20},{20,24},{24,28},{1,5},{5,9},{9,... | collective-permute-start | bytes 1327112 | tf_op jit(solution)/shard_map/ppermute | solution.py:11
  501.2 21.3 %collective-permute-start.14 = (bf16[1728,128]{1,0:T(8,128)(2,1)S(1)}, bf16[1728,128]{1,0:T(8,128)(2,1)S(1)}, u32[]{:S(2)}, u32[]{:S(2)}) collective-permute-start(bf16[1728,128]{1,0:T(8,128)(2,1)S(1)} %bitcast.179), channel_id=1, source_target_pairs={{4,0},{8,4},{12,8},{16,12},{20,16},{24,20},{28,24},{5,1},{9,5},{13... | collective-permute-start | bytes 1327112 | tf_op jit(solution)/shard_map/ppermute | solution.py:16
  515.6 19.4 %collective-permute-start.11 = (bf16[1728,128]{1,0:T(8,128)(2,1)S(1)}, bf16[1728,128]{1,0:T(8,128)(2,1)S(1)}, u32[]{:S(2)}, u32[]{:S(2)}) collective-permute-start(bf16[1728,128]{1,0:T(8,128)(2,1)S(1)} %bitcast.166), channel_id=1, source_target_pairs={{4,0},{8,4},{12,8},{16,12},{20,16},{24,20},{28,24},{5,1},{9,5},{13... | collective-permute-start | bytes 1327112 | tf_op jit(solution)/shard_map/ppermute | solution.py:16
  522.5 20.4 %collective-permute-start.7 = (bf16[1728,128]{1,0:T(8,128)(2,1)S(1)}, bf16[1728,128]{1,0:T(8,128)(2,1)S(1)}, u32[]{:S(2)}, u32[]{:S(2)}) collective-permute-start(bf16[1728,128]{1,0:T(8,128)(2,1)S(1)} %bitcast.170), channel_id=1, source_target_pairs={{0,4},{4,8},{8,12},{12,16},{16,20},{20,24},{24,28},{1,5},{5,9},{9,... | collective-permute-start | bytes 1327112 | tf_op jit(solution)/shard_map/ppermute | solution.py:11
  525.2 19.0 %collective-permute-start.8 = (bf16[1728,128]{1,0:T(8,128)(2,1)S(1)}, bf16[1728,128]{1,0:T(8,128)(2,1)S(1)}, u32[]{:S(2)}, u32[]{:S(2)}) collective-permute-start(bf16[1728,128]{1,0:T(8,128)(2,1)S(1)} %bitcast.171), channel_id=1, source_target_pairs={{4,0},{8,4},{12,8},{16,12},{20,16},{24,20},{28,24},{5,1},{9,5},{13... | collective-permute-start | bytes 1327112 | tf_op jit(solution)/shard_map/ppermute | solution.py:16
  537.4 19.5 %collective-permute-start.5 = (bf16[1728,128]{1,0:T(8,128)(2,1)S(1)}, bf16[1728,128]{1,0:T(8,128)(2,1)S(1)}, u32[]{:S(2)}, u32[]{:S(2)}) collective-permute-start(bf16[1728,128]{1,0:T(8,128)(2,1)S(1)} %bitcast.158), channel_id=1, source_target_pairs={{4,0},{8,4},{12,8},{16,12},{20,16},{24,20},{28,24},{5,1},{9,5},{13... | collective-permute-start | bytes 1327112 | tf_op jit(solution)/shard_map/ppermute | solution.py:16
  (55 other events, 1457.3 us)
Sparse Core Ops, SparseCore 0:
  15.8 50.5 all-gather.6
  67.9 49.3 all-gather.4
  119.6 39.4 reduce-scatter.22
  161.4 42.3 reduce-scatter.20
  206.0 51.6 reduce-scatter.18
  260.0 42.4 reduce-scatter.16
  304.8 42.2 reduce-scatter.14
  349.6 42.2 reduce-scatter.12
  394.2 42.2 reduce-scatter.10
  438.9 42.3 reduce-scatter.8

commit v2 on v1

v2 whole, which is shorter than its diff:
```python
import jax
import jax.numpy as jnp
from jax import lax
from jax.sharding import PartitionSpec as P

CHUNKS = 4
CORES = 2


def from_lower(values, axis):
    ends = lax.axis_size(axis) - 1
    return lax.ppermute(values, axis, [(i, i + 1) for i in range(ends)])


def from_higher(values, axis):
    ends = lax.axis_size(axis) - 1
    return lax.ppermute(values, axis, [(i + 1, i) for i in range(ends)])


def hop(values, axis, pairs):
    return lax.ppermute(values, axis, pairs)


def core_pairs(axis):
    return [(i, i + 1 - 2 * (i % CORES)) for i in range(lax.axis_size(axis))]


def scatter_line(own, axis):
    chips = lax.axis_size(axis) // CORES
    chip = lax.axis_index(axis) // CORES
    total = lax.dynamic_index_in_dim(own, chip, 0, keepdims=False).astype(jnp.float32)
    up = down = None
    for step in range(chips - 1):
        target = jnp.clip(chips - 1 - step + chip, 0, chips - 1)
        lower = jnp.clip(step - (chips - 1 - chip), 0, chips - 1)
        send_up = lax.dynamic_index_in_dim(own, target, 0, keepdims=False)
        send_down = lax.dynamic_index_in_dim(own, lower, 0, keepdims=False)
        if step:
            send_up = (send_up.astype(jnp.float32) + up.astype(jnp.float32)).astype(own.dtype)
            send_down = (send_down.astype(jnp.float32) + down.astype(jnp.float32)).astype(own.dtype)
        rising, falling = [], []
        for at in range(step + 1):
            mirror = chips - 1 - at
            for core in range(CORES):
                rising.append((at * CORES + core, (at + 1) * CORES + core))
                falling.append((mirror * CORES + core, (mirror - 1) * CORES + core))
        up = hop(send_up, axis, rising)
        down = hop(send_down, axis, falling)
    if up is not None:
        total = total + up.astype(jnp.float32) + down.astype(jnp.float32)
    return total.astype(own.dtype)


def shifted(values, step):
    edge = jnp.zeros_like(values[..., :1])
    if step > 0:
        return jnp.concatenate([edge, values[..., :-1]], axis=-1)
    return jnp.concatenate([values[..., 1:], edge], axis=-1)


def transport(center, neighbours, speeds, positive, fluid):
    middle = center.astype(jnp.float32)
    flux = jnp.zeros_like(middle)
    for component, (low, high) in enumerate(neighbours):
        upstream = jnp.where(positive[component][:, None, None], low, high).astype(jnp.float32)
        flux = flux + speeds[component][:, None, None] * (middle - upstream)
    return (middle - fluid[None] * flux).astype(jnp.bfloat16)


def on_device(distribution, collision, speeds, directions, cell_flags):
    velocities = collision.shape[0]
    chunk = velocities // CHUNKS
    planes = lax.all_gather(distribution, "vout", axis=0, tiled=True)
    planes = planes.reshape((planes.shape[0] // CORES, CORES) + planes.shape[1:])
    core = lax.rem(lax.axis_index("vin"), CORES)
    mine = lax.dynamic_index_in_dim(planes, core, 1, keepdims=False)
    theirs = lax.dynamic_index_in_dim(planes, 1 - core, 1, keepdims=False)
    fluid = (1 - cell_flags[0]).astype(jnp.float32)
    outs = []
    for part in range(CHUNKS):
        own = slice(part * chunk, (part + 1) * chunk)
        block = collision[own]
        spec = "vu,zuyx->zvyx"
        away = jnp.einsum(spec, block, theirs, preferred_element_type=jnp.float32)
        near = jnp.einsum(spec, block, mine, preferred_element_type=jnp.float32)
        got = hop(away.astype(jnp.bfloat16), "vin", core_pairs("vin"))
        both = (near + got.astype(jnp.float32)).astype(jnp.bfloat16)
        cells = scatter_line(both, "vin")
        before = from_lower(cells[:, -1:], "cell")
        after = from_higher(cells[:, :1], "cell")
        neighbours = (
            (shifted(cells, 1), shifted(cells, -1)),
            (
                jnp.concatenate([before, cells[:, :-1]], axis=1),
                jnp.concatenate([cells[:, 1:], after], axis=1),
            ),
            (from_lower(cells, "vin"), from_higher(cells, "vin")),
        )
        outs.append(transport(cells, neighbours, speeds[:, own], directions[:, own] == 1, fluid))
    return jnp.concatenate(outs, axis=0)[None]


def solution(mesh):
    return jax.shard_map(
        on_device,
        mesh=mesh,
        in_specs=(
            P("vout", "vin", "cell", None),
            P("vout", "vin"),
            P(None, "vout"),
            P(None, "vout"),
            P("vin", "cell", None),
        ),
        out_specs=P("vin", "vout", "cell", None),
        check_vma=False,
    )
```

time: 629 us -> 550 us (0.87)
  waiting for transfers between devices: 333 us -> 289 us
  local copies, waits for them, and re-layouts: 64.7 us -> 44.1 us
  other arithmetic: 34.9 us -> 16.3 us
  starting transfers between devices: 69 us -> 83.4 us
  matrix products: 102 us -> 92.6 us
    reduce_scatter x8 -> x0, waiting for transfers between devices: 240 us -> none  [on_device(): lax.psum_scatter(partial, 'vin', scatter_dimension=0, tiled=True)[0]]
    ppermute x0 -> x28, waiting for transfers between devices: none -> 170 us  [hop(): return lax.ppermute(values, axis, pairs)]
    ppermute x0 -> x28, starting transfers between devices: none -> 47.3 us  [hop(): return lax.ppermute(values, axis, pairs)]
    ppermute x12 -> x8, waiting for transfers between devices: 0.74 us -> 24 us  [from_higher(): return lax.ppermute(values, axis, [(i + 1, i) for i in range(ends)])]
    another operation x8 -> x0, other arithmetic: 22.3 us -> none  [on_device(): outs.append(jnp.stack(done, axis=1))]
    slice x14 -> x13, local copies, waits for them, and re-layouts: 26.6 us -> 5.01 us  [the longest x4 2.58 us: transport(): positive[component][:, None, None]]
    ppermute x12 -> x8, starting transfers between devices: 37.9 us -> 17.9 us  [from_lower(): return lax.ppermute(values, axis, [(i, i + 1) for i in range(ends)])]
    convert_element_type x1 -> x20, other arithmetic: 0.01 us -> 15.3 us  [the longest x4 10.1 us: transport(): return (middle - fluid[None] * flux).astype(jnp.bfloat16)]
  transfers between devices with their start and end apart: 34 -> 45, of which waited for: 10 -> 19; matrix products, arithmetic and copies ran while one was open for 23% -> 16% of each run, Pallas kernels for 0% -> 0%
where the time goes in v2:
time: 550 us; the launch traced here: 541 us
  waiting for transfers between devices  289 us (53%)
  matrix products  92.6 us (17%)
  starting transfers between devices  83.4 us (15%)
  local copies, waits for them, and re-layouts  44.1 us (8%)
  other arithmetic  16.3 us (3%)
  between operations  15.1 us (3%)
    ppermute x28, waiting for transfers between devices, hop(): return lax.ppermute(values, axis, pairs)  170 us
    all_gather x1, waiting for transfers between devices, on_device(): planes = lax.all_gather(distribution, 'vout', axis=0, tiled=True)  85.5 us
    dot_general x4, matrix products, on_device(): near = jnp.einsum(spec, block, mine, preferred_element_type=jnp.float32)  50.2 us
    ppermute x28, starting transfers between devices, hop(): return lax.ppermute(values, axis, pairs)  47.3 us
    dot_general x4, matrix products, on_device(): away = jnp.einsum(spec, block, theirs, preferred_element_type=jnp.float32)  42.5 us
    broadcast_in_dim x1, local copies, waits for them, and re-layouts, on_device(): return jnp.concatenate(outs, axis=0)[None]  30 us
    ppermute x8, waiting for transfers between devices, from_higher(): return lax.ppermute(values, axis, [(i + 1, i) for i in range(ends)])  24 us
    ppermute x8, starting transfers between devices, from_higher(): return lax.ppermute(values, axis, [(i + 1, i) for i in range(ends)])  18.2 us
  transfers between devices with their start and end apart: 45, of which 19 were waited for; matrix products, arithmetic and copies ran while one was open for 16% of the time, Pallas kernels for 0%

profile of v2, /device:TPU:8, one launch (start us, length us, event | category | flops | bytes accessed | tf_op | source)
XLA Modules:
  0.0 541.0 jit_solution(17836284486952160869)
XLA Ops:
  15.8 85.5 %all-gather.2.cloned.1.call-done = bf16[8,1728,2,128]{3,1,2,0:T(8,128)(2,1)} async-done(((bf16[4,1728,2,128]{3,1,2,0:T(8,128)(2,1)}), bf16[8,1728,2,128]{3,1,2,0:T(8,128)(2,1)}) %all-gather.2.cloned.1.call-update) | async-done | bytes 7077904 | tf_op jit(solution)/shard_map/all_gather | solution.py:73
  101.4 11.6 %fusion.71 = bf16[4,1728,2,128]{3,1,2,0:T(8,128)(2,1)} fusion(bf16[6912,1728]{0,1:T(8,128)(2,1)} %param.6, bf16[4,2,1728,2,128]{4,2,3,1,0:T(8,128)(2,1)} %bitcast.197, s32[]{:T(128)S(6)} %select_n.84), kind=kOutput, calls=%fused_computation.48 | convolution fusion | flops 6117064704 | bytes 13271044 | tf_op jit(solution)/shard_map/vu,zuyx->zvyx/dot_general | solution.py:84
  114.5 11.3 %fusion.66 = bf16[4,1728,2,128]{3,1,2,0:T(8,128)(2,1)} fusion(bf16[6912,1728]{0,1:T(8,128)(2,1)S(1)} %bitcast.196, bf16[4,2,1728,2,128]{4,2,3,1,0:T(8,128)(2,1)S(1)} %bitcast.202, s32[]{:T(128)S(6)} %select_n.84), kind=kOutput, calls=%fused_computation.47 | convolution fusion | flops 6117064704 | bytes 13271044 | tf_op jit(solution)/shard_map/vu,zuyx->zvyx/dot_general | solution.py:84
  126.4 8.1 %fusion.61 = bf16[4,1728,2,128]{3,1,2,0:T(8,128)(2,1)} fusion(bf16[6912,1728]{0,1:T(8,128)(2,1)S(1)} %bitcast.196, bf16[4,2,1728,2,128]{4,2,3,1,0:T(8,128)(2,1)S(1)} %bitcast.203, s32[]{:T(128)S(6)} %select_n.84), kind=kOutput, calls=%fused_computation.46 | convolution fusion | flops 6117064704 | bytes 13271044 | tf_op jit(solution)/shard_map/vu,zuyx->zvyx/dot_general | solution.py:84
  134.5 11.5 %fusion.56 = bf16[4,1728,2,128]{3,1,2,0:T(8,128)(2,1)} fusion(bf16[6912,1728]{0,1:T(8,128)(2,1)S(1)} %bitcast.196, bf16[4,2,1728,2,128]{4,2,3,1,0:T(8,128)(2,1)S(1)} %bitcast.204, s32[]{:T(128)S(6)} %select_n.84), kind=kOutput, calls=%fused_computation.45 | convolution fusion | flops 6117064704 | bytes 13271044 | tf_op jit(solution)/shard_map/vu,zuyx->zvyx/dot_general | solution.py:84
  146.5 10.7 %fusion.3 = bf16[4,1728,2,128]{3,1,2,0:T(8,128)(2,1)S(1)} fusion(bf16[4,1728,2,128]{3,1,2,0:T(8,128)(2,1)} %collective-permute-done, bf16[6912,1728]{0,1:T(8,128)(2,1)} %param.6, bf16[4,2,1728,2,128]{4,2,3,1,0:T(8,128)(2,1)} %bitcast.198, s32[]{:T(128)S(6)} %select_n.83), kind=kOutput, calls=%fused_computation.7 | convolution fusion | flops 6120603648 | bytes 16809988 | tf_op jit(solution)/shard_map/vu,zuyx->zvyx/dot_general | solution.py:85
  159.4 14.7 %fusion.2 = bf16[4,1728,2,128]{3,1,2,0:T(8,128)(2,1)S(1)} fusion(bf16[4,1728,2,128]{3,1,2,0:T(8,128)(2,1)} %collective-permute-done.11, bf16[6912,1728]{0,1:T(8,128)(2,1)} %param.6, bf16[4,2,1728,2,128]{4,2,3,1,0:T(8,128)(2,1)} %bitcast.199, s32[]{:T(128)S(6)} %select_n.83), kind=kOutput, calls=%fused_computation.5 | convolution fusion | flops 6120603648 | bytes 16809988 | tf_op jit(solution)/shard_map/vu,zuyx->zvyx/dot_general | solution.py:85
  178.1 10.7 %fusion.1 = bf16[4,1728,2,128]{3,1,2,0:T(8,128)(2,1)S(1)} fusion(bf16[4,1728,2,128]{3,1,2,0:T(8,128)(2,1)} %copy-done.29, bf16[6912,1728]{0,1:T(8,128)(2,1)} %param.6, bf16[4,2,1728,2,128]{4,2,3,1,0:T(8,128)(2,1)} %bitcast.200, s32[]{:T(128)S(6)} %select_n.83), kind=kOutput, calls=%fused_computation.3 | convolution fusion | flops 6120603648 | bytes 16809988 | tf_op jit(solution)/shard_map/vu,zuyx->zvyx/dot_general | solution.py:85
  190.3 14.0 %fusion = bf16[4,1728,2,128]{3,1,2,0:T(8,128)(2,1)S(1)} fusion(bf16[4,1728,2,128]{3,1,2,0:T(8,128)(2,1)S(1)} %collective-permute-done.33, bf16[6912,1728]{0,1:T(8,128)(2,1)} %param.6, bf16[4,2,1728,2,128]{4,2,3,1,0:T(8,128)(2,1)} %bitcast.201, s32[]{:T(128)S(6)} %select_n.83), kind=kOutput, calls=%fused_computation.1 | convolution fusion | flops 6120603648 | bytes 16809988 | tf_op jit(solution)/shard_map/vu,zuyx->zvyx/dot_general | solution.py:85
  207.0 12.7 %collective-permute-done.23 = bf16[1728,2,128]{2,0,1:T(8,128)(2,1)S(1)} collective-permute-done((bf16[1728,2,128]{2,0,1:T(8,128)(2,1)S(1)}, bf16[1728,2,128]{2,0,1:T(8,128)(2,1)S(1)}, u32[]{:S(2)}, u32[]{:S(2)}) %collective-permute-start.23) | collective-permute-done | bytes 884768 | tf_op jit(solution)/shard_map/ppermute | solution.py:21
  221.8 16.8 %collective-permute-done.34 = bf16[1728,2,128]{2,0,1:T(8,128)(2,1)S(1)} collective-permute-done((bf16[1728,2,128]{2,0,1:T(8,128)(2,1)S(1)}, bf16[1728,2,128]{2,0,1:T(8,128)(2,1)S(1)}, u32[]{:S(2)}, u32[]{:S(2)}) %collective-permute-start.34) | collective-permute-done | bytes 884768 | tf_op jit(solution)/shard_map/ppermute | solution.py:21
  241.5 16.1 %collective-permute-done.2 = bf16[1728,2,128]{2,0,1:T(8,128)(2,1)S(1)} collective-permute-done((bf16[1728,2,128]{2,0,1:T(8,128)(2,1)S(1)}, bf16[1728,2,128]{2,0,1:T(8,128)(2,1)S(1)}, u32[]{:S(2)}, u32[]{:S(2)}) %collective-permute-start.2) | collective-permute-done | bytes 884768 | tf_op jit(solution)/shard_map/ppermute | solution.py:21
  261.9 14.6 %collective-permute-done.13 = bf16[1728,2,128]{2,0,1:T(8,128)(2,1)S(1)} collective-permute-done((bf16[1728,2,128]{2,0,1:T(8,128)(2,1)S(1)}, bf16[1728,2,128]{2,0,1:T(8,128)(2,1)S(1)}, u32[]{:S(2)}, u32[]{:S(2)}) %collective-permute-start.13) | collective-permute-done | bytes 884768 | tf_op jit(solution)/shard_map/ppermute | solution.py:21
  282.9 12.6 %collective-permute-done.24 = bf16[1728,2,128]{2,0,1:T(8,128)(2,1)S(1)} collective-permute-done((bf16[1728,2,128]{2,0,1:T(8,128)(2,1)S(1)}, bf16[1728,2,128]{2,0,1:T(8,128)(2,1)S(1)}, u32[]{:S(2)}, u32[]{:S(2)}) %collective-permute-start.24) | collective-permute-done | bytes 884768 | tf_op jit(solution)/shard_map/ppermute | solution.py:21
  301.8 12.6 %collective-permute-done.35 = bf16[1728,2,128]{2,0,1:T(8,128)(2,1)S(1)} collective-permute-done((bf16[1728,2,128]{2,0,1:T(8,128)(2,1)S(1)}, bf16[1728,2,128]{2,0,1:T(8,128)(2,1)S(1)}, u32[]{:S(2)}, u32[]{:S(2)}) %collective-permute-start.35) | collective-permute-done | bytes 884768 | tf_op jit(solution)/shard_map/ppermute | solution.py:21
  322.6 16.3 %collective-permute-done.27 = bf16[1728,2,128]{2,0,1:T(8,128)(2,1)S(1)} collective-permute-done((bf16[1728,2,128]{2,0,1:T(8,128)(2,1)S(1)}, bf16[1728,2,128]{2,0,1:T(8,128)(2,1)S(1)}, u32[]{:S(2)}, u32[]{:S(2)}) %collective-permute-start.27) | collective-permute-done | bytes 884768 | tf_op jit(solution)/shard_map/ppermute | solution.py:21
  341.1 16.8 %collective-permute-done.38 = bf16[1728,2,128]{2,0,1:T(8,128)(2,1)S(1)} collective-permute-done((bf16[1728,2,128]{2,0,1:T(8,128)(2,1)S(1)}, bf16[1728,2,128]{2,0,1:T(8,128)(2,1)S(1)}, u32[]{:S(2)}, u32[]{:S(2)}) %collective-permute-start.38) | collective-permute-done | bytes 884768 | tf_op jit(solution)/shard_map/ppermute | solution.py:21
  364.0 12.8 %collective-permute-done.6 = bf16[1728,2,128]{2,0,1:T(8,128)(2,1)S(1)} collective-permute-done((bf16[1728,2,128]{2,0,1:T(8,128)(2,1)S(1)}, bf16[1728,2,128]{2,0,1:T(8,128)(2,1)S(1)}, u32[]{:S(2)}, u32[]{:S(2)}) %collective-permute-start.6) | collective-permute-done | bytes 884768 | tf_op jit(solution)/shard_map/ppermute | solution.py:21
  381.6 14.2 %collective-permute-done.17 = bf16[1728,2,128]{2,0,1:T(8,128)(2,1)S(1)} collective-permute-done((bf16[1728,2,128]{2,0,1:T(8,128)(2,1)S(1)}, bf16[1728,2,128]{2,0,1:T(8,128)(2,1)S(1)}, u32[]{:S(2)}, u32[]{:S(2)}) %collective-permute-start.17) | collective-permute-done | bytes 884768 | tf_op jit(solution)/shard_map/ppermute | solution.py:21
  400.9 13.9 %collective-permute-done.28 = bf16[1728,2,128]{2,0,1:T(8,128)(2,1)S(1)} collective-permute-done((bf16[1728,2,128]{2,0,1:T(8,128)(2,1)S(1)}, bf16[1728,2,128]{2,0,1:T(8,128)(2,1)S(1)}, u32[]{:S(2)}, u32[]{:S(2)}) %collective-permute-start.28) | collective-permute-done | bytes 884768 | tf_op jit(solution)/shard_map/ppermute | solution.py:21
  420.2 10.7 %collective-permute-done.39 = bf16[1728,2,128]{2,0,1:T(8,128)(2,1)S(1)} collective-permute-done((bf16[1728,2,128]{2,0,1:T(8,128)(2,1)S(1)}, bf16[1728,2,128]{2,0,1:T(8,128)(2,1)S(1)}, u32[]{:S(2)}, u32[]{:S(2)}) %collective-permute-start.39) | collective-permute-done | bytes 884768 | tf_op jit(solution)/shard_map/ppermute | solution.py:21
  442.6 11.0 %collective-permute-done.19 = bf16[1728,1,128]{2,0,1:T(8,128)(2,1)S(1)} collective-permute-done((bf16[1728,1,128]{2,0,1:T(8,128)(2,1)S(1)}, bf16[1728,1,128]{2,0,1:T(8,128)(2,1)S(1)}, u32[]{:S(2)}, u32[]{:S(2)}) %collective-permute-start.19) | collective-permute-done | bytes 442400 | tf_op jit(solution)/shard_map/ppermute | solution.py:17
  478.6 8.9 %collective-permute-done.30 = bf16[1728,1,128]{2,0,1:T(8,128)(2,1)S(1)} collective-permute-done((bf16[1728,1,128]{2,0,1:T(8,128)(2,1)S(1)}, bf16[1728,1,128]{2,0,1:T(8,128)(2,1)S(1)}, u32[]{:S(2)}, u32[]{:S(2)}) %collective-permute-start.30) | collective-permute-done | bytes 442400 | tf_op jit(solution)/shard_map/ppermute | solution.py:17
  503.6 30.0 %copy.20 = bf16[1,6912,2,128]{3,2,1,0:T(2,128)(2,1)} copy(bf16[1,6912,2,128]{3,1,2,0:T(8,128)(2,1)S(1)} %maximum_bitcast_fusion) | data formatting | bytes 7077888 | tf_op jit(solution)/shard_map/broadcast_in_dim | solution.py:100
  (190 shorter events, 127.6 us)
Async XLA Ops:
  6.5 94.8 %all-gather.2.cloned.1.call-start = ((), (), s32[]{:S(2)}) async-start(), calls=%async_computation | async-start | bytes 10616832 | tf_op jit(solution)/shard_map/all_gather | solution.py:73
  146.0 43.1 %collective-permute-start.33 = (bf16[4,1728,2,128]{3,1,2,0:T(8,128)(2,1)}, bf16[4,1728,2,128]{3,1,2,0:T(8,128)(2,1)S(1)}, u32[]{:S(2)}, u32[]{:S(2)}) collective-permute-start(bf16[4,1728,2,128]{3,1,2,0:T(8,128)(2,1)} %fusion.56), channel_id=1, source_target_pairs={{0,4},{4,0},{8,12},{12,8},{16,20},{20,16},{24,28},{28,24},{1,5},{5... | collective-permute-start | bytes 10616840 | tf_op jit(solution)/shard_map/ppermute | solution.py:21
  157.3 47.1 %collective-permute-start.1 = (bf16[1728,2,128]{2,0,1:T(8,128)(2,1)S(1)}, bf16[1728,2,128]{2,0,1:T(8,128)(2,1)S(1)}, u32[]{:S(2)}, u32[]{:S(2)}) collective-permute-start(bf16[1728,2,128]{2,0,1:T(8,128)(2,1)S(1)} %get-tuple-element.31), channel_id=1, source_target_pairs={{0,8},{4,12},{1,9},{5,13},{2,10},{6,14},{3,11},{7,15}} | collective-permute-start | bytes 2654216 | tf_op jit(solution)/shard_map/ppermute | solution.py:21
  158.6 82.1 %collective-permute-start.4 = (bf16[1728,2,128]{2,0,1:T(8,128)(2,1)S(1)}, bf16[1728,2,128]{2,0,1:T(8,128)(2,1)S(1)}, u32[]{:S(2)}, u32[]{:S(2)}) collective-permute-start(bf16[1728,2,128]{2,0,1:T(8,128)(2,1)S(1)} %get-tuple-element.32), channel_id=1, source_target_pairs={{24,16},{28,20},{25,17},{29,21},{26,18},{30,22},{27,19},{31,23}} | collective-permute-start | bytes 2654216 | tf_op jit(solution)/shard_map/ppermute | solution.py:21
  177.4 82.5 %collective-permute-start.15 = (bf16[1728,2,128]{2,0,1:T(8,128)(2,1)S(1)}, bf16[1728,2,128]{2,0,1:T(8,128)(2,1)S(1)}, u32[]{:S(2)}, u32[]{:S(2)}) collective-permute-start(bf16[1728,2,128]{2,0,1:T(8,128)(2,1)S(1)} %get-tuple-element.36), channel_id=1, source_target_pairs={{24,16},{28,20},{25,17},{29,21},{26,18},{30,22},{27,19},{31,23}} | collective-permute-start | bytes 2654216 | tf_op jit(solution)/shard_map/ppermute | solution.py:21
  204.5 73.9 %collective-permute-start.26 = (bf16[1728,2,128]{2,0,1:T(8,128)(2,1)S(1)}, bf16[1728,2,128]{2,0,1:T(8,128)(2,1)S(1)}, u32[]{:S(2)}, u32[]{:S(2)}) collective-permute-start(bf16[1728,2,128]{2,0,1:T(8,128)(2,1)S(1)} %get-tuple-element.40), channel_id=1, source_target_pairs={{24,16},{28,20},{25,17},{29,21},{26,18},{30,22},{27,19},{31,23}} | collective-permute-start | bytes 2654216 | tf_op jit(solution)/shard_map/ppermute | solution.py:21
  219.7 37.9 %collective-permute-start.2 = (bf16[1728,2,128]{2,0,1:T(8,128)(2,1)S(1)}, bf16[1728,2,128]{2,0,1:T(8,128)(2,1)S(1)}, u32[]{:S(2)}, u32[]{:S(2)}) collective-permute-start(bf16[1728,2,128]{2,0,1:T(8,128)(2,1)S(1)} %fusion.132), channel_id=1, source_target_pairs={{0,8},{4,12},{8,16},{12,20},{1,9},{5,13},{9,17},{13,21},{2,10},{6,... | collective-permute-start | bytes 2654216 | tf_op jit(solution)/shard_map/ppermute | solution.py:21
  238.6 37.9 %collective-permute-start.13 = (bf16[1728,2,128]{2,0,1:T(8,128)(2,1)S(1)}, bf16[1728,2,128]{2,0,1:T(8,128)(2,1)S(1)}, u32[]{:S(2)}, u32[]{:S(2)}) collective-permute-start(bf16[1728,2,128]{2,0,1:T(8,128)(2,1)S(1)} %fusion.126), channel_id=1, source_target_pairs={{0,8},{4,12},{8,16},{12,20},{1,9},{5,13},{9,17},{13,21},{2,10},{6,... | collective-permute-start | bytes 2654216 | tf_op jit(solution)/shard_map/ppermute | solution.py:21
  240.8 56.5 %collective-permute-start.37 = (bf16[1728,2,128]{2,0,1:T(8,128)(2,1)S(1)}, bf16[1728,2,128]{2,0,1:T(8,128)(2,1)S(1)}, u32[]{:S(2)}, u32[]{:S(2)}) collective-permute-start(bf16[1728,2,128]{2,0,1:T(8,128)(2,1)S(1)} %get-tuple-element.44), channel_id=1, source_target_pairs={{24,16},{28,20},{25,17},{29,21},{26,18},{30,22},{27,19},{31,23}} | collective-permute-start | bytes 2654216 | tf_op jit(solution)/shard_map/ppermute | solution.py:21
  257.6 37.9 %collective-permute-start.24 = (bf16[1728,2,128]{2,0,1:T(8,128)(2,1)S(1)}, bf16[1728,2,128]{2,0,1:T(8,128)(2,1)S(1)}, u32[]{:S(2)}, u32[]{:S(2)}) collective-permute-start(bf16[1728,2,128]{2,0,1:T(8,128)(2,1)S(1)} %fusion.120), channel_id=1, source_target_pairs={{0,8},{4,12},{8,16},{12,20},{1,9},{5,13},{9,17},{13,21},{2,10},{6,... | collective-permute-start | bytes 2654216 | tf_op jit(solution)/shard_map/ppermute | solution.py:21
  260.0 54.5 %collective-permute-start.35 = (bf16[1728,2,128]{2,0,1:T(8,128)(2,1)S(1)}, bf16[1728,2,128]{2,0,1:T(8,128)(2,1)S(1)}, u32[]{:S(2)}, u32[]{:S(2)}) collective-permute-start(bf16[1728,2,128]{2,0,1:T(8,128)(2,1)S(1)} %fusion.114), channel_id=1, source_target_pairs={{0,8},{4,12},{8,16},{12,20},{1,9},{5,13},{9,17},{13,21},{2,10},{6,... | collective-permute-start | bytes 2654216 | tf_op jit(solution)/shard_map/ppermute | solution.py:21
  276.5 39.7 %collective-permute-start.5 = (bf16[1728,2,128]{2,0,1:T(8,128)(2,1)S(1)}, bf16[1728,2,128]{2,0,1:T(8,128)(2,1)S(1)}, u32[]{:S(2)}, u32[]{:S(2)}) collective-permute-start(bf16[1728,2,128]{2,0,1:T(8,128)(2,1)S(1)} %get-tuple-element.30), channel_id=1, source_target_pairs={{24,16},{28,20},{16,8},{20,12},{25,17},{29,21},{17,9},{21,13},{26,... | collective-permute-start | bytes 2654216 | tf_op jit(solution)/shard_map/ppermute | solution.py:21
  278.3 81.7 %collective-permute-start.3 = (bf16[1728,2,128]{2,0,1:T(8,128)(2,1)S(1)}, bf16[1728,2,128]{2,0,1:T(8,128)(2,1)S(1)}, u32[]{:S(2)}, u32[]{:S(2)}) collective-permute-start(bf16[1728,2,128]{2,0,1:T(8,128)(2,1)S(1)} %get-tuple-element.29), channel_id=1, source_target_pairs={{0,8},{4,12},{8,16},{12,20},{16,24},{20,28},{1,9},{5,13},{9,17},{1... | collective-permute-start | bytes 2654216 | tf_op jit(solution)/shard_map/ppermute | solution.py:21
  297.3 82.4 %collective-permute-start.14 = (bf16[1728,2,128]{2,0,1:T(8,128)(2,1)S(1)}, bf16[1728,2,128]{2,0,1:T(8,128)(2,1)S(1)}, u32[]{:S(2)}, u32[]{:S(2)}) collective-permute-start(bf16[1728,2,128]{2,0,1:T(8,128)(2,1)S(1)} %get-tuple-element.33), channel_id=1, source_target_pairs={{0,8},{4,12},{8,16},{12,20},{16,24},{20,28},{1,9},{5,13},{9,17},{1... | collective-permute-start | bytes 2654216 | tf_op jit(solution)/shard_map/ppermute | solution.py:21
  316.2 82.3 %collective-permute-start.25 = (bf16[1728,2,128]{2,0,1:T(8,128)(2,1)S(1)}, bf16[1728,2,128]{2,0,1:T(8,128)(2,1)S(1)}, u32[]{:S(2)}, u32[]{:S(2)}) collective-permute-start(bf16[1728,2,128]{2,0,1:T(8,128)(2,1)S(1)} %get-tuple-element.37), channel_id=1, source_target_pairs={{0,8},{4,12},{8,16},{12,20},{16,24},{20,28},{1,9},{5,13},{9,17},{1... | collective-permute-start | bytes 2654216 | tf_op jit(solution)/shard_map/ppermute | solution.py:21
  321.0 36.8 %collective-permute-start.38 = (bf16[1728,2,128]{2,0,1:T(8,128)(2,1)S(1)}, bf16[1728,2,128]{2,0,1:T(8,128)(2,1)S(1)}, u32[]{:S(2)}, u32[]{:S(2)}) collective-permute-start(bf16[1728,2,128]{2,0,1:T(8,128)(2,1)S(1)} %get-tuple-element.42), channel_id=1, source_target_pairs={{24,16},{28,20},{16,8},{20,12},{25,17},{29,21},{17,9},{21,13},{26,... | collective-permute-start | bytes 2654216 | tf_op jit(solution)/shard_map/ppermute | solution.py:21
  338.9 37.9 %collective-permute-start.6 = (bf16[1728,2,128]{2,0,1:T(8,128)(2,1)S(1)}, bf16[1728,2,128]{2,0,1:T(8,128)(2,1)S(1)}, u32[]{:S(2)}, u32[]{:S(2)}) collective-permute-start(bf16[1728,2,128]{2,0,1:T(8,128)(2,1)S(1)} %fusion.131), channel_id=1, source_target_pairs={{24,16},{28,20},{16,8},{20,12},{8,0},{12,4},{25,17},{29,21},{17,9}... | collective-permute-start | bytes 2654216 | tf_op jit(solution)/shard_map/ppermute | solution.py:21
  357.9 61.0 %collective-permute-start.36 = (bf16[1728,2,128]{2,0,1:T(8,128)(2,1)S(1)}, bf16[1728,2,128]{2,0,1:T(8,128)(2,1)S(1)}, u32[]{:S(2)}, u32[]{:S(2)}) collective-permute-start(bf16[1728,2,128]{2,0,1:T(8,128)(2,1)S(1)} %get-tuple-element.41), channel_id=1, source_target_pairs={{0,8},{4,12},{8,16},{12,20},{16,24},{20,28},{1,9},{5,13},{9,17},{1... | collective-permute-start | bytes 2654216 | tf_op jit(solution)/shard_map/ppermute | solution.py:21
  376.8 37.9 %collective-permute-start.28 = (bf16[1728,2,128]{2,0,1:T(8,128)(2,1)S(1)}, bf16[1728,2,128]{2,0,1:T(8,128)(2,1)S(1)}, u32[]{:S(2)}, u32[]{:S(2)}) collective-permute-start(bf16[1728,2,128]{2,0,1:T(8,128)(2,1)S(1)} %fusion.119), channel_id=1, source_target_pairs={{24,16},{28,20},{16,8},{20,12},{8,0},{12,4},{25,17},{29,21},{17,9}... | collective-permute-start | bytes 2654216 | tf_op jit(solution)/shard_map/ppermute | solution.py:21
  379.7 51.3 %collective-permute-start.39 = (bf16[1728,2,128]{2,0,1:T(8,128)(2,1)S(1)}, bf16[1728,2,128]{2,0,1:T(8,128)(2,1)S(1)}, u32[]{:S(2)}, u32[]{:S(2)}) collective-permute-start(bf16[1728,2,128]{2,0,1:T(8,128)(2,1)S(1)} %fusion.113), channel_id=1, source_target_pairs={{24,16},{28,20},{16,8},{20,12},{8,0},{12,4},{25,17},{29,21},{17,9}... | collective-permute-start | bytes 2654216 | tf_op jit(solution)/shard_map/ppermute | solution.py:21
  395.8 59.6 %collective-permute-start.10 = (bf16[1728,2,128]{2,0,1:T(8,128)(2,1)S(1)}, bf16[1728,2,128]{2,0,1:T(8,128)(2,1)S(1)}, u32[]{:S(2)}, u32[]{:S(2)}) collective-permute-start(bf16[1728,2,128]{2,0,1:T(8,128)(2,1)S(1)} %fusion.135), channel_id=1, source_target_pairs={{4,0},{8,4},{12,8},{16,12},{20,16},{24,20},{28,24},{5,1},{9,5},{13... | collective-permute-start | bytes 2654216 | tf_op jit(solution)/shard_map/ppermute | solution.py:17
  398.5 60.6 %collective-permute-start.9 = (bf16[1728,2,128]{2,0,1:T(8,128)(2,1)S(1)}, bf16[1728,2,128]{2,0,1:T(8,128)(2,1)S(1)}, u32[]{:S(2)}, u32[]{:S(2)}) collective-permute-start(bf16[1728,2,128]{2,0,1:T(8,128)(2,1)S(1)} %fusion.135), channel_id=1, source_target_pairs={{0,4},{4,8},{8,12},{12,16},{16,20},{20,24},{24,28},{1,5},{5,9},{9,... | collective-permute-start | bytes 2654216 | tf_op jit(solution)/shard_map/ppermute | solution.py:12
  435.2 35.8 %collective-permute-start.20 = (bf16[1728,2,128]{2,0,1:T(8,128)(2,1)S(1)}, bf16[1728,2,128]{2,0,1:T(8,128)(2,1)S(1)}, u32[]{:S(2)}, u32[]{:S(2)}) collective-permute-start(bf16[1728,2,128]{2,0,1:T(8,128)(2,1)S(1)} %fusion.129), channel_id=1, source_target_pairs={{0,4},{4,8},{8,12},{12,16},{16,20},{20,24},{24,28},{1,5},{5,9},{9,... | collective-permute-start | bytes 2654216 | tf_op jit(solution)/shard_map/ppermute | solution.py:12
  437.1 37.5 %collective-permute-start.21 = (bf16[1728,2,128]{2,0,1:T(8,128)(2,1)S(1)}, bf16[1728,2,128]{2,0,1:T(8,128)(2,1)S(1)}, u32[]{:S(2)}, u32[]{:S(2)}) collective-permute-start(bf16[1728,2,128]{2,0,1:T(8,128)(2,1)S(1)} %fusion.129), channel_id=1, source_target_pairs={{4,0},{8,4},{12,8},{16,12},{20,16},{24,20},{28,24},{5,1},{9,5},{13... | collective-permute-start | bytes 2654216 | tf_op jit(solution)/shard_map/ppermute | solution.py:17
  (57 other events, 1104.2 us)
Sparse Core Ops, SparseCore 0:
  10.9 90.3 all-gather.1

commit v3 on v2

--- a/solution.py
+++ b/solution.py
@@ -3,7 +3,7 @@
 from jax import lax
 from jax.sharding import PartitionSpec as P
 
-CHUNKS = 4
+CHUNKS = 3
 CORES = 2
 
 

time: 550 us -> 513 us (0.933)
  local copies, waits for them, and re-layouts: 44.1 us -> 12.8 us
  waiting for transfers between devices: 289 us -> 317 us
  starting transfers between devices: 83.4 us -> 61.7 us
  matrix products: 92.6 us -> 83 us
    broadcast_in_dim x1, local copies, waits for them, and re-layouts: 30 us -> 6.53 us  [on_device(): return jnp.concatenate(outs, axis=0)[None]]
    ppermute x28 -> x21, waiting for transfers between devices: 170 us -> 180 us  [hop(): return lax.ppermute(values, axis, pairs)]
    ppermute x28 -> x21, starting transfers between devices: 47.3 us -> 37.8 us  [hop(): return lax.ppermute(values, axis, pairs)]
    dot_general x4 -> x3, matrix products: 50.2 us -> 40.9 us  [on_device(): near = jnp.einsum(spec, block, mine, preferred_element_type=jnp.float32)]
    ppermute x8 -> x6, waiting for transfers between devices: 9.64 us -> 18 us  [from_lower(): return lax.ppermute(values, axis, [(i, i + 1) for i in range(ends)])]
    ppermute x8 -> x6, starting transfers between devices: 18.2 us -> 11.3 us  [from_higher(): return lax.ppermute(values, axis, [(i + 1, i) for i in range(ends)])]
    ppermute x8 -> x6, starting transfers between devices: 17.9 us -> 12.6 us  [from_lower(): return lax.ppermute(values, axis, [(i, i + 1) for i in range(ends)])]
    ppermute x8 -> x6, waiting for transfers between devices: 24 us -> 28.7 us  [from_higher(): return lax.ppermute(values, axis, [(i + 1, i) for i in range(ends)])]
  transfers between devices with their start and end apart: 45 -> 34, of which waited for: 19 -> 16; matrix products, arithmetic and copies ran while one was open for 16% -> 17% of each run, Pallas kernels for 0% -> 0%
where the time goes in v3:
time: 513 us; the launch traced here: 505 us
  waiting for transfers between devices  317 us (62%)
  matrix products  83 us (16%)
  starting transfers between devices  61.7 us (12%)
  other arithmetic  15.7 us (3%)
  between operations  14.4 us (3%)
  local copies, waits for them, and re-layouts  12.8 us (2%)
    ppermute x21, waiting for transfers between devices, hop(): return lax.ppermute(values, axis, pairs)  180 us
    all_gather x1, waiting for transfers between devices, on_device(): planes = lax.all_gather(distribution, 'vout', axis=0, tiled=True)  90.5 us
    dot_general x3, matrix products, on_device(): away = jnp.einsum(spec, block, theirs, preferred_element_type=jnp.float32)  42.1 us
    dot_general x3, matrix products, on_device(): near = jnp.einsum(spec, block, mine, preferred_element_type=jnp.float32)  40.9 us
    ppermute x21, starting transfers between devices, hop(): return lax.ppermute(values, axis, pairs)  37.8 us
    ppermute x6, waiting for transfers between devices, from_higher(): return lax.ppermute(values, axis, [(i + 1, i) for i in range(ends)])  28.7 us
    ppermute x6, waiting for transfers between devices, from_lower(): return lax.ppermute(values, axis, [(i, i + 1) for i in range(ends)])  18 us
    ppermute x6, starting transfers between devices, from_lower(): return lax.ppermute(values, axis, [(i, i + 1) for i in range(ends)])  12.6 us
  transfers between devices with their start and end apart: 34, of which 16 were waited for; matrix products, arithmetic and copies ran while one was open for 17% of the time, Pallas kernels for 0%

profile of v3, /device:TPU:8, one launch (start us, length us, event | category | flops | bytes accessed | tf_op | source)
XLA Modules:
  0.0 504.8 jit_solution(819726647843778147)
XLA Ops:
  10.8 90.5 %all-gather.2.cloned.1.call-done = bf16[8,1728,2,128]{3,1,2,0:T(8,128)(2,1)} async-done(((bf16[4,1728,2,128]{3,1,2,0:T(8,128)(2,1)}), bf16[8,1728,2,128]{3,1,2,0:T(8,128)(2,1)}) %all-gather.2.cloned.1.call-update) | async-done | bytes 7077904 | tf_op jit(solution)/shard_map/all_gather | solution.py:73
  101.4 14.5 %fusion.42 = bf16[4,2304,2,128]{1,3,2,0:T(8,128)(2,1)} fusion(bf16[6912,1728]{0,1:T(8,128)(2,1)} %param.6, bf16[4,2,1728,2,128]{4,2,3,1,0:T(8,128)(2,1)} %bitcast.137, s32[]{:T(128)S(6)} %select_n.67), kind=kOutput, calls=%fused_computation.29 | convolution fusion | flops 8156086272 | bytes 16220164 | tf_op jit(solution)/shard_map/vu,zuyx->zvyx/dot_general | solution.py:84
  115.9 13.7 %fusion.39 = bf16[4,2304,2,128]{1,3,2,0:T(8,128)(2,1)} fusion(bf16[6912,1728]{0,1:T(8,128)(2,1)} %param.6, bf16[4,2,1728,2,128]{4,2,3,1,0:T(8,128)(2,1)S(1)} %bitcast.141, s32[]{:T(128)S(6)} %select_n.67), kind=kOutput, calls=%fused_computation.28 | convolution fusion | flops 8156086272 | bytes 16220164 | tf_op jit(solution)/shard_map/vu,zuyx->zvyx/dot_general | solution.py:84
  130.1 13.9 %fusion.36 = bf16[4,2304,2,128]{1,3,2,0:T(8,128)(2,1)} fusion(bf16[6912,1728]{0,1:T(8,128)(2,1)} %param.6, bf16[4,2,1728,2,128]{4,2,3,1,0:T(8,128)(2,1)S(1)} %bitcast.142, s32[]{:T(128)S(6)} %select_n.67), kind=kOutput, calls=%fused_computation.27 | convolution fusion | flops 8156086272 | bytes 16220164 | tf_op jit(solution)/shard_map/vu,zuyx->zvyx/dot_general | solution.py:84
  144.7 13.6 %fusion.2 = bf16[4,2304,2,128]{1,3,2,0:T(8,128)(2,1)S(1)} fusion(bf16[4,2304,2,128]{1,3,2,0:T(8,128)(2,1)} %collective-permute-done, bf16[6912,1728]{0,1:T(8,128)(2,1)} %param.6, bf16[4,2,1728,2,128]{4,2,3,1,0:T(8,128)(2,1)} %bitcast.138, s32[]{:T(128)S(6)} %select_n.66), kind=kOutput, calls=%fused_computation.5 | convolution fusion | flops 8160804864 | bytes 20938756 | tf_op jit(solution)/shard_map/vu,zuyx->zvyx/dot_general | solution.py:85
  161.4 13.8 %fusion.1 = bf16[4,2304,2,128]{1,3,2,0:T(8,128)(2,1)S(1)} fusion(bf16[4,2304,2,128]{1,3,2,0:T(8,128)(2,1)} %collective-permute-done.11, bf16[6912,1728]{0,1:T(8,128)(2,1)} %param.6, bf16[4,2,1728,2,128]{4,2,3,1,0:T(8,128)(2,1)} %bitcast.139, s32[]{:T(128)S(6)} %select_n.66), kind=kOutput, calls=%fused_computation.3 | convolution fusion | flops 8160804864 | bytes 20938756 | tf_op jit(solution)/shard_map/vu,zuyx->zvyx/dot_general | solution.py:85
  178.3 13.6 %fusion = bf16[4,2304,2,128]{1,3,2,0:T(8,128)(2,1)S(1)} fusion(bf16[4,2304,2,128]{1,3,2,0:T(8,128)(2,1)} %collective-permute-done.22, bf16[6912,1728]{0,1:T(8,128)(2,1)} %param.6, bf16[4,2,1728,2,128]{4,2,3,1,0:T(8,128)(2,1)} %bitcast.140, s32[]{:T(128)S(6)} %select_n.66), kind=kOutput, calls=%fused_computation.1 | convolution fusion | flops 8160804864 | bytes 20938756 | tf_op jit(solution)/shard_map/vu,zuyx->zvyx/dot_general | solution.py:85
  194.4 20.1 %collective-permute-done.12 = bf16[2304,2,128]{0,2,1:T(8,128)(2,1)} collective-permute-done((bf16[2304,2,128]{0,2,1:T(8,128)(2,1)S(1)}, bf16[2304,2,128]{0,2,1:T(8,128)(2,1)}, u32[]{:S(2)}, u32[]{:S(2)}) %collective-permute-start.12) | collective-permute-done | bytes 1179680 | tf_op jit(solution)/shard_map/ppermute | solution.py:21
  218.0 21.7 %collective-permute-done.23 = bf16[2304,2,128]{0,2,1:T(8,128)(2,1)S(1)} collective-permute-done((bf16[2304,2,128]{0,2,1:T(8,128)(2,1)S(1)}, bf16[2304,2,128]{0,2,1:T(8,128)(2,1)S(1)}, u32[]{:S(2)}, u32[]{:S(2)}) %collective-permute-start.23) | collective-permute-done | bytes 1179680 | tf_op jit(solution)/shard_map/ppermute | solution.py:21
  243.8 21.1 %collective-permute-done.2 = bf16[2304,2,128]{0,2,1:T(8,128)(2,1)S(1)} collective-permute-done((bf16[2304,2,128]{0,2,1:T(8,128)(2,1)S(1)}, bf16[2304,2,128]{0,2,1:T(8,128)(2,1)S(1)}, u32[]{:S(2)}, u32[]{:S(2)}) %collective-permute-start.2) | collective-permute-done | bytes 1179680 | tf_op jit(solution)/shard_map/ppermute | solution.py:21
  268.1 4.8 collective-permute-start.3
  272.9 17.3 %collective-permute-done.13 = bf16[2304,2,128]{0,2,1:T(8,128)(2,1)S(1)} collective-permute-done((bf16[2304,2,128]{0,2,1:T(8,128)(2,1)S(1)}, bf16[2304,2,128]{0,2,1:T(8,128)(2,1)S(1)}, u32[]{:S(2)}, u32[]{:S(2)}) %collective-permute-start.13) | collective-permute-done | bytes 1179680 | tf_op jit(solution)/shard_map/ppermute | solution.py:21
  293.4 4.6 collective-permute-start.14
  297.9 17.5 %collective-permute-done.24 = bf16[2304,2,128]{0,2,1:T(8,128)(2,1)S(1)} collective-permute-done((bf16[2304,2,128]{0,2,1:T(8,128)(2,1)S(1)}, bf16[2304,2,128]{0,2,1:T(8,128)(2,1)S(1)}, u32[]{:S(2)}, u32[]{:S(2)}) %collective-permute-start.24) | collective-permute-done | bytes 1179680 | tf_op jit(solution)/shard_map/ppermute | solution.py:21
  317.4 4.6 collective-permute-start.25
  324.6 23.0 %collective-permute-done.27 = bf16[2304,2,128]{0,2,1:T(8,128)(2,1)S(1)} collective-permute-done((bf16[2304,2,128]{0,2,1:T(8,128)(2,1)S(1)}, bf16[2304,2,128]{0,2,1:T(8,128)(2,1)S(1)}, u32[]{:S(2)}, u32[]{:S(2)}) %collective-permute-start.27) | collective-permute-done | bytes 1179680 | tf_op jit(solution)/shard_map/ppermute | solution.py:21
  351.8 21.1 %collective-permute-done.6 = bf16[2304,2,128]{0,2,1:T(8,128)(2,1)S(1)} collective-permute-done((bf16[2304,2,128]{0,2,1:T(8,128)(2,1)S(1)}, bf16[2304,2,128]{0,2,1:T(8,128)(2,1)S(1)}, u32[]{:S(2)}, u32[]{:S(2)}) %collective-permute-start.6) | collective-permute-done | bytes 1179680 | tf_op jit(solution)/shard_map/ppermute | solution.py:21
  378.0 20.2 %collective-permute-done.17 = bf16[2304,2,128]{0,2,1:T(8,128)(2,1)S(1)} collective-permute-done((bf16[2304,2,128]{0,2,1:T(8,128)(2,1)S(1)}, bf16[2304,2,128]{0,2,1:T(8,128)(2,1)S(1)}, u32[]{:S(2)}, u32[]{:S(2)}) %collective-permute-start.17) | collective-permute-done | bytes 1179680 | tf_op jit(solution)/shard_map/ppermute | solution.py:21
  404.4 17.9 %collective-permute-done.28 = bf16[2304,2,128]{0,2,1:T(8,128)(2,1)S(1)} collective-permute-done((bf16[2304,2,128]{0,2,1:T(8,128)(2,1)S(1)}, bf16[2304,2,128]{0,2,1:T(8,128)(2,1)S(1)}, u32[]{:S(2)}, u32[]{:S(2)}) %collective-permute-start.28) | collective-permute-done | bytes 1179680 | tf_op jit(solution)/shard_map/ppermute | solution.py:21
  426.3 12.0 %collective-permute-done.8 = bf16[2304,1,128]{0,2,1:T(8,128)(2,1)S(1)} collective-permute-done((bf16[2304,1,128]{0,2,1:T(8,128)(2,1)S(1)}, bf16[2304,1,128]{0,2,1:T(8,128)(2,1)S(1)}, u32[]{:S(2)}, u32[]{:S(2)}) %collective-permute-start.8) | collective-permute-done | bytes 589856 | tf_op jit(solution)/shard_map/ppermute | solution.py:17
  439.8 10.7 %collective-permute-done.18 = bf16[2304,1,128]{0,2,1:T(8,128)(2,1)S(1)} collective-permute-done((bf16[2304,1,128]{0,2,1:T(8,128)(2,1)S(1)}, bf16[2304,1,128]{0,2,1:T(8,128)(2,1)S(1)}, u32[]{:S(2)}, u32[]{:S(2)}) %collective-permute-start.18) | collective-permute-done | bytes 589856 | tf_op jit(solution)/shard_map/ppermute | solution.py:12
  459.6 12.5 %collective-permute-done.19 = bf16[2304,1,128]{0,2,1:T(8,128)(2,1)S(1)} collective-permute-done((bf16[2304,1,128]{0,2,1:T(8,128)(2,1)S(1)}, bf16[2304,1,128]{0,2,1:T(8,128)(2,1)S(1)}, u32[]{:S(2)}, u32[]{:S(2)}) %collective-permute-start.19) | collective-permute-done | bytes 589856 | tf_op jit(solution)/shard_map/ppermute | solution.py:17
  477.1 7.3 %collective-permute-done.29 = bf16[2304,1,128]{0,2,1:T(8,128)(2,1)S(1)} collective-permute-done((bf16[2304,1,128]{0,2,1:T(8,128)(2,1)S(1)}, bf16[2304,1,128]{0,2,1:T(8,128)(2,1)S(1)}, u32[]{:S(2)}, u32[]{:S(2)}) %collective-permute-start.29) | collective-permute-done | bytes 589856 | tf_op jit(solution)/shard_map/ppermute | solution.py:12
  491.0 6.5 %copy.12 = bf16[1,6912,2,128]{3,2,1,0:T(2,128)(2,1)} copy(bf16[1,6912,2,128]{1,3,2,0:T(8,128)(2,1)S(1)} %maximum_bitcast_fusion) | data formatting | bytes 7077888 | tf_op jit(solution)/shard_map/broadcast_in_dim | solution.py:100
  (92 shorter events, 74.1 us)
Async XLA Ops:
  6.5 94.8 %all-gather.2.cloned.1.call-start = ((), (), s32[]{:S(2)}) async-start(), calls=%async_computation | async-start | bytes 10616832 | tf_op jit(solution)/shard_map/all_gather | solution.py:73
  144.0 34.4 %collective-permute-start.22 = (bf16[4,2304,2,128]{1,3,2,0:T(8,128)(2,1)}, bf16[4,2304,2,128]{1,3,2,0:T(8,128)(2,1)}, u32[]{:S(2)}, u32[]{:S(2)}) collective-permute-start(bf16[4,2304,2,128]{1,3,2,0:T(8,128)(2,1)} %fusion.36), channel_id=1, source_target_pairs={{0,4},{4,0},{8,12},{12,8},{16,20},{20,16},{24,28},{28,24},{1,5},{5... | collective-permute-start | bytes 14155784 | tf_op jit(solution)/shard_map/ppermute | solution.py:21
  158.4 35.0 %collective-permute-start.1 = (bf16[2304,2,128]{0,2,1:T(8,128)(2,1)S(1)}, bf16[2304,2,128]{0,2,1:T(8,128)(2,1)S(1)}, u32[]{:S(2)}, u32[]{:S(2)}) collective-permute-start(bf16[2304,2,128]{0,2,1:T(8,128)(2,1)S(1)} %get-tuple-element.25), channel_id=1, source_target_pairs={{0,8},{4,12},{1,9},{5,13},{2,10},{6,14},{3,11},{7,15}} | collective-permute-start | bytes 3538952 | tf_op jit(solution)/shard_map/ppermute | solution.py:21
  159.7 82.2 %collective-permute-start.4 = (bf16[2304,2,128]{0,2,1:T(8,128)(2,1)S(1)}, bf16[2304,2,128]{0,2,1:T(8,128)(2,1)}, u32[]{:S(2)}, u32[]{:S(2)}) collective-permute-start(bf16[2304,2,128]{0,2,1:T(8,128)(2,1)S(1)} %get-tuple-element.26), channel_id=1, source_target_pairs={{24,16},{28,20},{25,17},{29,21},{26,18},{30,22},{27,19},{31,23}} | collective-permute-start | bytes 3538952 | tf_op jit(solution)/shard_map/ppermute | solution.py:21
  175.3 39.1 %collective-permute-start.12 = (bf16[2304,2,128]{0,2,1:T(8,128)(2,1)S(1)}, bf16[2304,2,128]{0,2,1:T(8,128)(2,1)}, u32[]{:S(2)}, u32[]{:S(2)}) collective-permute-start(bf16[2304,2,128]{0,2,1:T(8,128)(2,1)S(1)} %get-tuple-element.29), channel_id=1, source_target_pairs={{0,8},{4,12},{1,9},{5,13},{2,10},{6,14},{3,11},{7,15}} | collective-permute-start | bytes 3538952 | tf_op jit(solution)/shard_map/ppermute | solution.py:21
  176.6 91.5 %collective-permute-start.15 = (bf16[2304,2,128]{0,2,1:T(8,128)(2,1)S(1)}, bf16[2304,2,128]{0,2,1:T(8,128)(2,1)}, u32[]{:S(2)}, u32[]{:S(2)}) collective-permute-start(bf16[2304,2,128]{0,2,1:T(8,128)(2,1)S(1)} %get-tuple-element.30), channel_id=1, source_target_pairs={{24,16},{28,20},{25,17},{29,21},{26,18},{30,22},{27,19},{31,23}} | collective-permute-start | bytes 3538952 | tf_op jit(solution)/shard_map/ppermute | solution.py:21
  192.1 47.6 %collective-permute-start.23 = (bf16[2304,2,128]{0,2,1:T(8,128)(2,1)S(1)}, bf16[2304,2,128]{0,2,1:T(8,128)(2,1)S(1)}, u32[]{:S(2)}, u32[]{:S(2)}) collective-permute-start(bf16[2304,2,128]{0,2,1:T(8,128)(2,1)S(1)} %get-tuple-element.33), channel_id=1, source_target_pairs={{0,8},{4,12},{1,9},{5,13},{2,10},{6,14},{3,11},{7,15}} | collective-permute-start | bytes 3538952 | tf_op jit(solution)/shard_map/ppermute | solution.py:21
  193.4 100.0 %collective-permute-start.26 = (bf16[2304,2,128]{0,2,1:T(8,128)(2,1)S(1)}, bf16[2304,2,128]{0,2,1:T(8,128)(2,1)S(1)}, u32[]{:S(2)}, u32[]{:S(2)}) collective-permute-start(bf16[2304,2,128]{0,2,1:T(8,128)(2,1)S(1)} %get-tuple-element.34), channel_id=1, source_target_pairs={{24,16},{28,20},{25,17},{29,21},{26,18},{30,22},{27,19},{31,23}} | collective-permute-start | bytes 3538952 | tf_op jit(solution)/shard_map/ppermute | solution.py:21
  214.5 50.5 %collective-permute-start.2 = (bf16[2304,2,128]{0,2,1:T(8,128)(2,1)S(1)}, bf16[2304,2,128]{0,2,1:T(8,128)(2,1)S(1)}, u32[]{:S(2)}, u32[]{:S(2)}) collective-permute-start(bf16[2304,2,128]{0,2,1:T(8,128)(2,1)S(1)} %fusion.92), channel_id=1, source_target_pairs={{0,8},{4,12},{8,16},{12,20},{1,9},{5,13},{9,17},{13,21},{2,10},{6,... | collective-permute-start | bytes 3538952 | tf_op jit(solution)/shard_map/ppermute | solution.py:21
  239.6 50.6 %collective-permute-start.13 = (bf16[2304,2,128]{0,2,1:T(8,128)(2,1)S(1)}, bf16[2304,2,128]{0,2,1:T(8,128)(2,1)S(1)}, u32[]{:S(2)}, u32[]{:S(2)}) collective-permute-start(bf16[2304,2,128]{0,2,1:T(8,128)(2,1)S(1)} %fusion.86), channel_id=1, source_target_pairs={{0,8},{4,12},{8,16},{12,20},{1,9},{5,13},{9,17},{13,21},{2,10},{6,... | collective-permute-start | bytes 3538952 | tf_op jit(solution)/shard_map/ppermute | solution.py:21
  241.9 73.6 %collective-permute-start.24 = (bf16[2304,2,128]{0,2,1:T(8,128)(2,1)S(1)}, bf16[2304,2,128]{0,2,1:T(8,128)(2,1)S(1)}, u32[]{:S(2)}, u32[]{:S(2)}) collective-permute-start(bf16[2304,2,128]{0,2,1:T(8,128)(2,1)S(1)} %fusion.80), channel_id=1, source_target_pairs={{0,8},{4,12},{8,16},{12,20},{1,9},{5,13},{9,17},{13,21},{2,10},{6,... | collective-permute-start | bytes 3538952 | tf_op jit(solution)/shard_map/ppermute | solution.py:21
  266.8 50.6 %collective-permute-start.5 = (bf16[2304,2,128]{0,2,1:T(8,128)(2,1)S(1)}, bf16[2304,2,128]{0,2,1:T(8,128)(2,1)S(1)}, u32[]{:S(2)}, u32[]{:S(2)}) collective-permute-start(bf16[2304,2,128]{0,2,1:T(8,128)(2,1)S(1)} %get-tuple-element.24), channel_id=1, source_target_pairs={{24,16},{28,20},{16,8},{20,12},{25,17},{29,21},{17,9},{21,13},{26,... | collective-permute-start | bytes 3538952 | tf_op jit(solution)/shard_map/ppermute | solution.py:21
  268.1 81.7 %collective-permute-start.3 = (bf16[2304,2,128]{0,2,1:T(8,128)(2,1)S(1)}, bf16[2304,2,128]{0,2,1:T(8,128)(2,1)S(1)}, u32[]{:S(2)}, u32[]{:S(2)}) collective-permute-start(bf16[2304,2,128]{0,2,1:T(8,128)(2,1)S(1)} %get-tuple-element.23), channel_id=1, source_target_pairs={{0,8},{4,12},{8,16},{12,20},{16,24},{20,28},{1,9},{5,13},{9,17},{1... | collective-permute-start | bytes 3538952 | tf_op jit(solution)/shard_map/ppermute | solution.py:21
  293.4 82.2 %collective-permute-start.14 = (bf16[2304,2,128]{0,2,1:T(8,128)(2,1)S(1)}, bf16[2304,2,128]{0,2,1:T(8,128)(2,1)S(1)}, u32[]{:S(2)}, u32[]{:S(2)}) collective-permute-start(bf16[2304,2,128]{0,2,1:T(8,128)(2,1)S(1)} %get-tuple-element.27), channel_id=1, source_target_pairs={{0,8},{4,12},{8,16},{12,20},{16,24},{20,28},{1,9},{5,13},{9,17},{1... | collective-permute-start | bytes 3538952 | tf_op jit(solution)/shard_map/ppermute | solution.py:21
  317.4 83.6 %collective-permute-start.25 = (bf16[2304,2,128]{0,2,1:T(8,128)(2,1)S(1)}, bf16[2304,2,128]{0,2,1:T(8,128)(2,1)S(1)}, u32[]{:S(2)}, u32[]{:S(2)}) collective-permute-start(bf16[2304,2,128]{0,2,1:T(8,128)(2,1)S(1)} %get-tuple-element.31), channel_id=1, source_target_pairs={{0,8},{4,12},{8,16},{12,20},{16,24},{20,28},{1,9},{5,13},{9,17},{1... | collective-permute-start | bytes 3538952 | tf_op jit(solution)/shard_map/ppermute | solution.py:21
  322.3 50.6 %collective-permute-start.6 = (bf16[2304,2,128]{0,2,1:T(8,128)(2,1)S(1)}, bf16[2304,2,128]{0,2,1:T(8,128)(2,1)S(1)}, u32[]{:S(2)}, u32[]{:S(2)}) collective-permute-start(bf16[2304,2,128]{0,2,1:T(8,128)(2,1)S(1)} %fusion.91), channel_id=1, source_target_pairs={{24,16},{28,20},{16,8},{20,12},{8,0},{12,4},{25,17},{29,21},{17,9}... | collective-permute-start | bytes 3538952 | tf_op jit(solution)/shard_map/ppermute | solution.py:21
  347.6 50.6 %collective-permute-start.17 = (bf16[2304,2,128]{0,2,1:T(8,128)(2,1)S(1)}, bf16[2304,2,128]{0,2,1:T(8,128)(2,1)S(1)}, u32[]{:S(2)}, u32[]{:S(2)}) collective-permute-start(bf16[2304,2,128]{0,2,1:T(8,128)(2,1)S(1)} %fusion.85), channel_id=1, source_target_pairs={{24,16},{28,20},{16,8},{20,12},{8,0},{12,4},{25,17},{29,21},{17,9}... | collective-permute-start | bytes 3538952 | tf_op jit(solution)/shard_map/ppermute | solution.py:21
  349.8 72.4 %collective-permute-start.28 = (bf16[2304,2,128]{0,2,1:T(8,128)(2,1)S(1)}, bf16[2304,2,128]{0,2,1:T(8,128)(2,1)S(1)}, u32[]{:S(2)}, u32[]{:S(2)}) collective-permute-start(bf16[2304,2,128]{0,2,1:T(8,128)(2,1)S(1)} %fusion.79), channel_id=1, source_target_pairs={{24,16},{28,20},{16,8},{20,12},{8,0},{12,4},{25,17},{29,21},{17,9}... | collective-permute-start | bytes 3538952 | tf_op jit(solution)/shard_map/ppermute | solution.py:21
  373.4 79.0 %collective-permute-start.10 = (bf16[2304,2,128]{0,2,1:T(8,128)(2,1)S(1)}, bf16[2304,2,128]{0,2,1:T(8,128)(2,1)S(1)}, u32[]{:S(2)}, u32[]{:S(2)}) collective-permute-start(bf16[2304,2,128]{0,2,1:T(8,128)(2,1)S(1)} %fusion.95), channel_id=1, source_target_pairs={{4,0},{8,4},{12,8},{16,12},{20,16},{24,20},{28,24},{5,1},{9,5},{13... | collective-permute-start | bytes 3538952 | tf_op jit(solution)/shard_map/ppermute | solution.py:17
  375.6 80.5 %collective-permute-start.9 = (bf16[2304,2,128]{0,2,1:T(8,128)(2,1)S(1)}, bf16[2304,2,128]{0,2,1:T(8,128)(2,1)S(1)}, u32[]{:S(2)}, u32[]{:S(2)}) collective-permute-start(bf16[2304,2,128]{0,2,1:T(8,128)(2,1)S(1)} %fusion.95), channel_id=1, source_target_pairs={{0,4},{4,8},{8,12},{12,16},{16,20},{20,24},{24,28},{1,5},{5,9},{9,... | collective-permute-start | bytes 3538952 | tf_op jit(solution)/shard_map/ppermute | solution.py:12
  398.6 74.9 %collective-permute-start.20 = (bf16[2304,2,128]{0,2,1:T(8,128)(2,1)S(1)}, bf16[2304,2,128]{0,2,1:T(8,128)(2,1)S(1)}, u32[]{:S(2)}, u32[]{:S(2)}) collective-permute-start(bf16[2304,2,128]{0,2,1:T(8,128)(2,1)S(1)} %fusion.89), channel_id=1, source_target_pairs={{0,4},{4,8},{8,12},{12,16},{16,20},{20,24},{24,28},{1,5},{5,9},{9,... | collective-permute-start | bytes 3538952 | tf_op jit(solution)/shard_map/ppermute | solution.py:12
  424.3 50.6 %collective-permute-start.21 = (bf16[2304,2,128]{0,2,1:T(8,128)(2,1)S(1)}, bf16[2304,2,128]{0,2,1:T(8,128)(2,1)S(1)}, u32[]{:S(2)}, u32[]{:S(2)}) collective-permute-start(bf16[2304,2,128]{0,2,1:T(8,128)(2,1)S(1)} %fusion.89), channel_id=1, source_target_pairs={{4,0},{8,4},{12,8},{16,12},{20,16},{24,20},{28,24},{5,1},{9,5},{13... | collective-permute-start | bytes 3538952 | tf_op jit(solution)/shard_map/ppermute | solution.py:17
  450.5 38.1 %collective-permute-start.31 = (bf16[2304,2,128]{0,2,1:T(8,128)(2,1)S(1)}, bf16[2304,2,128]{0,2,1:T(8,128)(2,1)S(1)}, u32[]{:S(2)}, u32[]{:S(2)}) collective-permute-start(bf16[2304,2,128]{0,2,1:T(8,128)(2,1)S(1)} %fusion.83), channel_id=1, source_target_pairs={{0,4},{4,8},{8,12},{12,16},{16,20},{20,24},{24,28},{1,5},{5,9},{9,... | collective-permute-start | bytes 3538952 | tf_op jit(solution)/shard_map/ppermute | solution.py:12
  452.4 36.1 %collective-permute-start.32 = (bf16[2304,2,128]{0,2,1:T(8,128)(2,1)S(1)}, bf16[2304,2,128]{0,2,1:T(8,128)(2,1)S(1)}, u32[]{:S(2)}, u32[]{:S(2)}) collective-permute-start(bf16[2304,2,128]{0,2,1:T(8,128)(2,1)S(1)} %fusion.83), channel_id=1, source_target_pairs={{4,0},{8,4},{12,8},{16,12},{20,16},{24,20},{28,24},{5,1},{9,5},{13... | collective-permute-start | bytes 3538952 | tf_op jit(solution)/shard_map/ppermute | solution.py:17
  (14 other events, 276.0 us)
Sparse Core Ops, SparseCore 0:
  10.9 90.3 all-gather.1
